TPU v7x, 32 devices: a whole 2x2x4 slice. The times are simulated.
32 devices in a mesh: dp: 8 (over y, x, core), gen: 4 (over z).
Axes of the slice: x: 2, y: 2, z: 4, core: 2. Of those that a mesh axis runs over, the one named last changes fastest.
Arguments:
- enc_input: bfloat16 [32, 512, 768], P(('dp', 'gen')), may hold values from -6 to 6
- dec_input: bfloat16 [32, 512, 768], P(('dp', 'gen')), may hold values from -6 to 6
- enc_segments: int32 [32, 512], P(('dp', 'gen')), may hold values from 0 to 3, never falling along the last dimension, each value on 1 to 256 neighbouring positions
- dec_segments: int32 [32, 512], P(('dp', 'gen')), may hold values from 0 to 3, never falling along the last dimension, each value on 1 to 256 neighbouring positions
- task_ids: int32 [32], P(('dp', 'gen')), may hold values from 0 to 7
- cotangent: bfloat16 [32, 512, 768], P(('dp', 'gen')), may hold values from -6 to 6
- enc_norms: bfloat16 [2, 768], replicated, may hold values from 0.5 to 1.5
- enc_qkv: bfloat16 [768, 2304], replicated, may hold values from -0.21875 to 0.21875
- enc_proj: bfloat16 [768, 768], replicated, may hold values from -0.875 to 0.875
- enc_up: bfloat16 [768, 3072], replicated, may hold values from -0.21875 to 0.21875
- enc_down: bfloat16 [3072, 768], replicated, may hold values from -0.109375 to 0.109375
- dec_norms: bfloat16 [4, 768], replicated, may hold values from 0.5 to 1.5
- dec_qkv: bfloat16 [768, 2304], replicated, may hold values from -0.21875 to 0.21875
- dec_self_proj: bfloat16 [768, 768], replicated, may hold values from -0.875 to 0.875
- dec_cross_q: bfloat16 [768, 768], replicated, may hold values from -0.21875 to 0.21875
- dec_cross_kv: bfloat16 [768, 1536], replicated, may hold values from -0.21875 to 0.21875
- dec_cross_proj: bfloat16 [768, 768], replicated, may hold values from -0.875 to 0.875
- dec_up: bfloat16 [768, 3072], replicated, may hold values from -0.21875 to 0.21875
- dec_down: bfloat16 [3072, 768], replicated, may hold values from -0.109375 to 0.109375
- task_emb: float32 [8, 64], replicated, may hold values from -6 to 6
- layer_emb: float32 [2, 128], replicated, may hold values from -6 to 6
- proj_task: float32 [64, 128], replicated, may hold values from -0.75 to 0.75
- gen_weight: bfloat16 [128, 48, 768], P(None, None, 'gen'), may hold values from -0.01953125 to 0.01953125
- gen_vector: bfloat16 [128, 3, 768], P(None, None, 'gen'), may hold values from -0.125 to 0.125
Outputs:
- dec_out: bfloat16 [32, 512, 768], P(('dp', 'gen'))
- enc_input_grad: bfloat16 [32, 512, 768], P(('dp', 'gen'))
- dec_input_grad: bfloat16 [32, 512, 768], P(('dp', 'gen'))
- enc_norms_grad: float32 [2, 768], P(None, 'dp')
- enc_qkv_grad: float32 [768, 2304], P('dp')
- enc_proj_grad: float32 [768, 768], P('dp')
- enc_up_grad: float32 [768, 3072], P('dp')
- enc_down_grad: float32 [3072, 768], P('dp')
- dec_norms_grad: float32 [4, 768], P(None, 'dp')
- dec_qkv_grad: float32 [768, 2304], P('dp')
- dec_self_proj_grad: float32 [768, 768], P('dp')
- dec_cross_q_grad: float32 [768, 768], P('dp')
- dec_cross_kv_grad: float32 [768, 1536], P('dp')
- dec_cross_proj_grad: float32 [768, 768], P('dp')
- dec_up_grad: float32 [768, 3072], P('dp')
- dec_down_grad: float32 [3072, 768], P('dp')
- task_emb_grad: float32 [8, 64], replicated
- layer_emb_grad: float32 [2, 128], replicated
- proj_task_grad: float32 [64, 128], replicated
- gen_weight_grad: float32 [128, 48, 768], P(None, None, 'gen')
- gen_vector_grad: float32 [128, 3, 768], P(None, None, 'gen')
Inputs may be any that keep to these rules, and one draw needn't show every extreme that they name: `enc_segments`: segment numbers never fall along a row; each row holds all 4 numbers, each on at most 256 positions. `dec_segments`: segment numbers never fall along a row; each row holds all 4 numbers, each on at most 256 positions.
All inputs are finite; a program needn't handle non-finite values.
Results may differ from a plain program's by a relative error of at most 0.025.
Values may be sent and summed in bfloat16 or wider, within the bound.
A program may use at most 320 MiB of HBM per device.

v0:
```python
import jax
import jax.numpy as jnp
from jax import lax
from jax.sharding import PartitionSpec as P

H = 12
HD = 64


HIGHEST = lax.Precision.HIGHEST


def product(left_side, right_side):
    return jnp.dot(left_side, right_side, preferred_element_type=jnp.float32)


def product_left(left_side, right_side):
    return lax.dot_general(
        left_side, right_side, (((0,), (0,)), ((), ())), preferred_element_type=jnp.float32
    )


def product_right(left_side, right_side):
    return lax.dot_general(
        left_side, right_side, (((1,), (1,)), ((), ())), preferred_element_type=jnp.float32
    )


def rms_norm(values, norm_gain):
    return values * lax.rsqrt(jnp.mean(values * values, axis=-1, keepdims=True) + 1e-06) * norm_gain


def layer_norm(values, norm_gain, norm_shift):
    centred = values - jnp.mean(values, axis=-1, keepdims=True)
    return (
        centred * lax.rsqrt(jnp.mean(centred * centred, axis=-1, keepdims=True) + 1e-05) * norm_gain
        + norm_shift
    )


def gelu_exact(values):
    return jax.nn.gelu(values, approximate=False)


def to_heads(matrix, row_count):
    return matrix.reshape(row_count, -1, H, HD)


def same_segment(seg_query, seg_key):
    return seg_query[:, None] == seg_key[None, :]


def causal_segment(seg_query, seg_key):
    places = jnp.arange(seg_query.shape[0])
    return same_segment(seg_query, seg_key) & (places[:, None] >= places[None, :])


def scores_of(queries, key_set, allowed):
    raw_scores = jnp.einsum("qhd,khd->hqk", queries, key_set, preferred_element_type=jnp.float32)
    return jnp.where(allowed[None], raw_scores * HD ** (-0.5), -1e30)


def attend_forward(queries, key_set, value_set, seg_query, seg_key, allowed_fn):

    def one_row(row_items):
        query_row, key_row, value_row, seg_q_row, seg_k_row = row_items
        scores = scores_of(query_row, key_row, allowed_fn(seg_q_row, seg_k_row))
        score_top = jnp.max(scores, axis=-1, keepdims=True)
        raised = jnp.exp(scores - score_top)
        row_total = jnp.sum(raised, axis=-1, keepdims=True)
        probs_low = (raised / row_total).astype(jnp.bfloat16)
        mixed_out = jnp.einsum(
            "hqk,khd->qhd", probs_low, value_row, preferred_element_type=jnp.float32
        )
        return (mixed_out.astype(jnp.bfloat16), score_top + jnp.log(row_total))

    return lax.map(one_row, (queries, key_set, value_set, seg_query, seg_key))


def attend_backward(
    queries, key_set, value_set, grad_mixed, log_total, seg_query, seg_key, allowed_fn
):

    def one_row(row_items):
        query_row, key_row, value_row, grad_row, log_row, seg_q_row, seg_k_row = row_items
        scores = scores_of(query_row, key_row, allowed_fn(seg_q_row, seg_k_row))
        probs = jnp.exp(scores - log_row)
        grad_probs = jnp.einsum(
            "qhd,khd->hqk", grad_row, value_row, preferred_element_type=jnp.float32
        )
        grad_scores = (
            probs * (grad_probs - jnp.sum(probs * grad_probs, axis=-1, keepdims=True))
        ).astype(jnp.bfloat16)
        scale_factor = HD ** (-0.5)
        grad_query = (
            jnp.einsum("hqk,khd->qhd", grad_scores, key_row, preferred_element_type=jnp.float32)
            * scale_factor
        )
        grad_key = (
            jnp.einsum("hqk,qhd->khd", grad_scores, query_row, preferred_element_type=jnp.float32)
            * scale_factor
        )
        grad_value = jnp.einsum(
            "hqk,qhd->khd", probs.astype(jnp.bfloat16), grad_row, preferred_element_type=jnp.float32
        )
        return (grad_query, grad_key, grad_value)

    return lax.map(
        one_row, (queries, key_set, value_set, grad_mixed, log_total, seg_query, seg_key)
    )


def attention_forward(normed, w_joint, segments, allowed_fn, row_count):
    model_width = w_joint.shape[0]
    normed_low = normed.astype(jnp.bfloat16)
    joint_proj = product(normed_low, w_joint).astype(jnp.bfloat16)
    queries = to_heads(joint_proj[:, :model_width], row_count)
    key_set = to_heads(joint_proj[:, model_width : 2 * model_width], row_count)
    value_set = to_heads(joint_proj[:, 2 * model_width :], row_count)
    mixed_out, log_total = attend_forward(
        queries, key_set, value_set, segments, segments, allowed_fn
    )
    return (
        mixed_out.reshape(-1, model_width),
        (normed_low, queries, key_set, value_set, log_total),
    )


def attention_backward(grad_mixed, stored, w_joint, segments, allowed_fn, row_count):
    normed_low, queries, key_set, value_set, log_total = stored
    model_width = w_joint.shape[0]
    grad_query, grad_key, grad_value = attend_backward(
        queries,
        key_set,
        value_set,
        to_heads(grad_mixed, row_count),
        log_total,
        segments,
        segments,
        allowed_fn,
    )
    grad_joint = jnp.concatenate(
        [
            grad_query.reshape(-1, model_width),
            grad_key.reshape(-1, model_width),
            grad_value.reshape(-1, model_width),
        ],
        axis=1,
    ).astype(jnp.bfloat16)
    return (product_right(grad_joint, w_joint), product_left(normed_low, grad_joint))


def output_backward(grad_hidden, mixed_flat, w_output):
    grad_low = grad_hidden.astype(jnp.bfloat16)
    return (
        product_right(grad_low, w_output).astype(jnp.bfloat16),
        product_left(mixed_flat, grad_low),
    )


def ffn_forward(normed, w_up, w_down):
    normed_low = normed.astype(jnp.bfloat16)
    before = product(normed_low, w_up)
    hidden = gelu_exact(before).astype(jnp.bfloat16)
    return (product(hidden, w_down), (normed_low, before, hidden))


def ffn_backward(grad_result, stored, w_up, w_down):
    normed_low, before, hidden = stored
    grad_low = grad_result.astype(jnp.bfloat16)
    grad_down = product_left(hidden, grad_low)
    grad_hidden = product_right(grad_low, w_down)
    grad_before = jax.vjp(gelu_exact, before)[1](grad_hidden)[0].astype(jnp.bfloat16)
    grad_up = product_left(normed_low, grad_before)
    return (product_right(grad_before, w_up), grad_up, grad_down)


def adapter_forward(values, weights, vectors):
    bottleneck = weights.shape[1] // 2
    normed_low = layer_norm(values, 1.0 + vectors[:, 1:2], vectors[:, 2:3]).astype(jnp.bfloat16)
    inner_pre = jnp.einsum(
        "rld,rad->rla", normed_low, weights[:, :bottleneck], preferred_element_type=jnp.float32
    )
    active_low = gelu_exact(inner_pre).astype(jnp.bfloat16)
    up_scale = (values.shape[-1] / bottleneck) ** 0.5
    result = (
        jnp.einsum(
            "rla,rad->rld", active_low, weights[:, bottleneck:], preferred_element_type=jnp.float32
        )
        * up_scale
        + vectors[:, 0:1]
    )
    return (result, (normed_low, inner_pre, active_low))


def adapter_backward(grad_result, values, weights, vectors, stored):
    normed_low, inner_pre, active_low = stored
    bottleneck = weights.shape[1] // 2
    up_scale = (values.shape[-1] / bottleneck) ** 0.5
    grad_low = (grad_result * up_scale).astype(jnp.bfloat16)
    grad_upper = jnp.einsum(
        "rla,rld->rad", active_low, grad_low, preferred_element_type=jnp.float32
    )
    grad_active = jnp.einsum(
        "rld,rad->rla", grad_low, weights[:, bottleneck:], preferred_element_type=jnp.float32
    )
    grad_inner = jax.vjp(gelu_exact, inner_pre)[1](grad_active)[0].astype(jnp.bfloat16)
    grad_lower = jnp.einsum(
        "rla,rld->rad", grad_inner, normed_low, preferred_element_type=jnp.float32
    )
    grad_normed = jnp.einsum(
        "rla,rad->rld", grad_inner, weights[:, :bottleneck], preferred_element_type=jnp.float32
    )
    norm_pull = jax.vjp(layer_norm, values, 1.0 + vectors[:, 1:2], vectors[:, 2:3])[1]
    grad_values, grad_gain, grad_shift = norm_pull(grad_normed)
    grad_weights = jnp.concatenate([grad_lower, grad_upper], axis=1)
    grad_vectors = jnp.concatenate(
        [jnp.sum(grad_result, axis=1, keepdims=True), grad_gain, grad_shift], axis=1
    )
    return (grad_values, grad_weights, grad_vectors)


def body(
    enc_input,
    dec_input,
    enc_segments,
    dec_segments,
    task_ids,
    cotangent,
    enc_norms,
    enc_qkv,
    enc_proj,
    enc_up,
    enc_down,
    dec_norms,
    dec_qkv,
    dec_self_proj,
    dec_cross_q,
    dec_cross_kv,
    dec_cross_proj,
    dec_up,
    dec_down,
    task_emb,
    layer_emb,
    proj_task,
    gen_weight,
    gen_vector,
):
    row_count, length, model_width = enc_input.shape
    layer_count = layer_emb.shape[0]
    pair_count = task_emb.shape[0] * layer_count
    tokens = row_count * length

    def source_of(task_table, layer_table, projection):
        mixed_in = (
            jnp.dot(task_table, projection, precision=HIGHEST)[:, None, :] + layer_table[None, :, :]
        )
        return gelu_exact(mixed_in).reshape(pair_count, -1)

    source, source_pull = jax.vjp(source_of, task_emb, layer_emb, proj_task)
    source_low = source.astype(jnp.bfloat16)
    piece_weights = jnp.einsum(
        "th,hkd->tkd", source_low, gen_weight, preferred_element_type=jnp.float32
    ).astype(jnp.bfloat16)
    piece_vectors = jnp.einsum(
        "th,hkd->tkd", source_low, gen_vector, preferred_element_type=jnp.float32
    ).astype(jnp.bfloat16)
    full_weights, full_vectors = (
        lax.all_gather(piece_weights, "gen", axis=2, tiled=True),
        lax.all_gather(piece_vectors, "gen", axis=2, tiled=True),
    )

    def select(layer_index):
        pair_index = task_ids * layer_count + layer_index
        picked = (pair_index[:, None] == jnp.arange(pair_count)[None, :]).astype(jnp.bfloat16)
        chosen_weights = jnp.einsum(
            "rt,tkd->rkd", picked, full_weights, preferred_element_type=jnp.float32
        ).astype(jnp.bfloat16)
        chosen_vectors = jnp.einsum(
            "rt,tkd->rkd", picked, full_vectors, preferred_element_type=jnp.float32
        )
        return (picked.astype(jnp.float32), chosen_weights, chosen_vectors)

    enc_rows = enc_input.astype(jnp.float32).reshape(tokens, model_width)
    enc_attn_in, enc_attn_pull = jax.vjp(rms_norm, enc_rows, enc_norms[0].astype(jnp.float32))
    enc_mixed, enc_attn_stored = attention_forward(
        enc_attn_in, enc_qkv, enc_segments, same_segment, row_count
    )
    enc_hidden = enc_rows + product(enc_mixed, enc_proj)
    enc_ffn_in, enc_ffn_pull = jax.vjp(rms_norm, enc_hidden, enc_norms[1].astype(jnp.float32))
    enc_ffn, enc_ffn_stored = ffn_forward(enc_ffn_in, enc_up, enc_down)
    picked_first, weights_first, vectors_first = select(0)
    enc_ffn_rows = enc_ffn.reshape(row_count, length, model_width)
    enc_adapted, enc_adapt_stored = adapter_forward(enc_ffn_rows, weights_first, vectors_first)
    encoded = enc_hidden + enc_ffn + enc_adapted.reshape(tokens, model_width)
    dec_rows = dec_input.astype(jnp.float32).reshape(tokens, model_width)
    dec_attn_in, dec_attn_pull = jax.vjp(rms_norm, dec_rows, dec_norms[0].astype(jnp.float32))
    dec_mixed, dec_attn_stored = attention_forward(
        dec_attn_in, dec_qkv, dec_segments, causal_segment, row_count
    )
    dec_hidden = dec_rows + product(dec_mixed, dec_self_proj)
    cross_in, cross_pull = jax.vjp(rms_norm, dec_hidden, dec_norms[1].astype(jnp.float32))
    memory_in, memory_pull = jax.vjp(rms_norm, encoded, dec_norms[3].astype(jnp.float32))
    cross_low = cross_in.astype(jnp.bfloat16)
    memory_low = memory_in.astype(jnp.bfloat16)
    cross_queries = to_heads(product(cross_low, dec_cross_q).astype(jnp.bfloat16), row_count)
    memory_proj = product(memory_low, dec_cross_kv).astype(jnp.bfloat16)
    memory_keys = to_heads(memory_proj[:, :model_width], row_count)
    memory_values = to_heads(memory_proj[:, model_width:], row_count)
    cross_out, cross_log = attend_forward(
        cross_queries, memory_keys, memory_values, dec_segments, enc_segments, same_segment
    )
    cross_flat = cross_out.reshape(tokens, model_width)
    cross_hidden = dec_hidden + product(cross_flat, dec_cross_proj)
    dec_ffn_in, dec_ffn_pull = jax.vjp(rms_norm, cross_hidden, dec_norms[2].astype(jnp.float32))
    dec_ffn, dec_ffn_stored = ffn_forward(dec_ffn_in, dec_up, dec_down)
    picked_second, weights_second, vectors_second = select(1)
    dec_ffn_rows = dec_ffn.reshape(row_count, length, model_width)
    dec_adapted, dec_adapt_stored = adapter_forward(dec_ffn_rows, weights_second, vectors_second)
    decoded = cross_hidden + dec_ffn + dec_adapted.reshape(tokens, model_width)
    grad_out = cotangent.astype(jnp.float32).reshape(tokens, model_width)
    grad_adapt_dec, grad_weights_second, grad_vectors_second = adapter_backward(
        grad_out.reshape(row_count, length, model_width),
        dec_ffn_rows,
        weights_second,
        vectors_second,
        dec_adapt_stored,
    )
    grad_dec_ffn_in, grad_dec_up, grad_dec_down = ffn_backward(
        grad_out + grad_adapt_dec.reshape(tokens, model_width), dec_ffn_stored, dec_up, dec_down
    )
    grad_from_dec_ffn, grad_gain_ffn = dec_ffn_pull(grad_dec_ffn_in)
    grad_cross_hidden = grad_out + grad_from_dec_ffn
    grad_cross_mixed, grad_dec_cross_proj = output_backward(
        grad_cross_hidden, cross_flat, dec_cross_proj
    )
    grad_query, grad_key, grad_value = attend_backward(
        cross_queries,
        memory_keys,
        memory_values,
        to_heads(grad_cross_mixed, row_count),
        cross_log,
        dec_segments,
        enc_segments,
        same_segment,
    )
    grad_query_low = grad_query.reshape(tokens, model_width).astype(jnp.bfloat16)
    grad_memory_low = jnp.concatenate(
        [grad_key.reshape(tokens, model_width), grad_value.reshape(tokens, model_width)], axis=1
    ).astype(jnp.bfloat16)
    grad_dec_cross_q = product_left(cross_low, grad_query_low)
    grad_dec_cross_kv = product_left(memory_low, grad_memory_low)
    grad_from_cross, grad_gain_cross = cross_pull(product_right(grad_query_low, dec_cross_q))
    grad_encoded, grad_gain_memory = memory_pull(product_right(grad_memory_low, dec_cross_kv))
    grad_dec_hidden = grad_cross_hidden + grad_from_cross
    grad_dec_mixed, grad_dec_self_proj = output_backward(grad_dec_hidden, dec_mixed, dec_self_proj)
    grad_dec_normed, grad_dec_qkv = attention_backward(
        grad_dec_mixed, dec_attn_stored, dec_qkv, dec_segments, causal_segment, row_count
    )
    grad_from_self, grad_gain_self = dec_attn_pull(grad_dec_normed)
    grad_dec_rows = grad_dec_hidden + grad_from_self
    grad_dec_norms = jnp.stack([grad_gain_self, grad_gain_cross, grad_gain_ffn, grad_gain_memory])
    grad_adapt_enc, grad_weights_first, grad_vectors_first = adapter_backward(
        grad_encoded.reshape(row_count, length, model_width),
        enc_ffn_rows,
        weights_first,
        vectors_first,
        enc_adapt_stored,
    )
    grad_enc_ffn_in, grad_enc_up, grad_enc_down = ffn_backward(
        grad_encoded + grad_adapt_enc.reshape(tokens, model_width), enc_ffn_stored, enc_up, enc_down
    )
    grad_from_enc_ffn, grad_gain_enc_ffn = enc_ffn_pull(grad_enc_ffn_in)
    grad_enc_hidden = grad_encoded + grad_from_enc_ffn
    grad_enc_mixed, grad_enc_proj = output_backward(grad_enc_hidden, enc_mixed, enc_proj)
    grad_enc_normed, grad_enc_qkv = attention_backward(
        grad_enc_mixed, enc_attn_stored, enc_qkv, enc_segments, same_segment, row_count
    )
    grad_from_enc_attn, grad_gain_enc_attn = enc_attn_pull(grad_enc_normed)
    grad_enc_rows = grad_enc_hidden + grad_from_enc_attn
    grad_enc_norms = jnp.stack([grad_gain_enc_attn, grad_gain_enc_ffn])
    grad_pairs_weights = jnp.einsum(
        "rt,rkd->tkd", picked_first, grad_weights_first, precision=HIGHEST
    ) + jnp.einsum("rt,rkd->tkd", picked_second, grad_weights_second, precision=HIGHEST)
    grad_pairs_vectors = jnp.einsum(
        "rt,rkd->tkd", picked_first, grad_vectors_first, precision=HIGHEST
    ) + jnp.einsum("rt,rkd->tkd", picked_second, grad_vectors_second, precision=HIGHEST)
    slice_weights, slice_vectors = (
        lax.psum_scatter(
            grad_pairs_weights.astype(jnp.bfloat16), "gen", scatter_dimension=2, tiled=True
        ).astype(jnp.float32),
        lax.psum_scatter(
            grad_pairs_vectors.astype(jnp.bfloat16), "gen", scatter_dimension=2, tiled=True
        ).astype(jnp.float32),
    )
    source_wide = source_low.astype(jnp.float32)
    weight_wide = gen_weight.astype(jnp.float32)
    vector_wide = gen_vector.astype(jnp.float32)
    part_weight = jnp.einsum("th,tkd->hkd", source_wide, slice_weights, precision=HIGHEST)
    part_vector = jnp.einsum("th,tkd->hkd", source_wide, slice_vectors, precision=HIGHEST)
    part_source = jnp.einsum(
        "tkd,hkd->th", slice_weights, weight_wide, precision=HIGHEST
    ) + jnp.einsum("tkd,hkd->th", slice_vectors, vector_wide, precision=HIGHEST)
    grad_gen_weight, grad_gen_vector = (
        lax.psum(part_weight.astype(jnp.bfloat16), "dp").astype(jnp.float32),
        lax.psum(part_vector.astype(jnp.bfloat16), "dp").astype(jnp.float32),
    )
    grad_source = lax.psum(part_source, ("dp", "gen"))
    grad_task_emb, grad_layer_emb, grad_proj_task = source_pull(grad_source)
    (
        grad_enc_norms,
        grad_enc_qkv,
        grad_enc_proj,
        grad_enc_up,
        grad_enc_down,
        grad_dec_norms,
        grad_dec_qkv,
        grad_dec_self_proj,
        grad_dec_cross_q,
        grad_dec_cross_kv,
        grad_dec_cross_proj,
        grad_dec_up,
        grad_dec_down,
    ) = (
        lax.psum_scatter(
            grad_enc_norms.astype(jnp.bfloat16), "dp", scatter_dimension=1, tiled=True
        ).astype(jnp.float32),
        lax.psum_scatter(
            grad_enc_qkv.astype(jnp.bfloat16), "dp", scatter_dimension=0, tiled=True
        ).astype(jnp.float32),
        lax.psum_scatter(
            grad_enc_proj.astype(jnp.bfloat16), "dp", scatter_dimension=0, tiled=True
        ).astype(jnp.float32),
        lax.psum_scatter(
            grad_enc_up.astype(jnp.bfloat16), "dp", scatter_dimension=0, tiled=True
        ).astype(jnp.float32),
        lax.psum_scatter(
            grad_enc_down.astype(jnp.bfloat16), "dp", scatter_dimension=0, tiled=True
        ).astype(jnp.float32),
        lax.psum_scatter(
            grad_dec_norms.astype(jnp.bfloat16), "dp", scatter_dimension=1, tiled=True
        ).astype(jnp.float32),
        lax.psum_scatter(
            grad_dec_qkv.astype(jnp.bfloat16), "dp", scatter_dimension=0, tiled=True
        ).astype(jnp.float32),
        lax.psum_scatter(
            grad_dec_self_proj.astype(jnp.bfloat16), "dp", scatter_dimension=0, tiled=True
        ).astype(jnp.float32),
        lax.psum_scatter(
            grad_dec_cross_q.astype(jnp.bfloat16), "dp", scatter_dimension=0, tiled=True
        ).astype(jnp.float32),
        lax.psum_scatter(
            grad_dec_cross_kv.astype(jnp.bfloat16), "dp", scatter_dimension=0, tiled=True
        ).astype(jnp.float32),
        lax.psum_scatter(
            grad_dec_cross_proj.astype(jnp.bfloat16), "dp", scatter_dimension=0, tiled=True
        ).astype(jnp.float32),
        lax.psum_scatter(
            grad_dec_up.astype(jnp.bfloat16), "dp", scatter_dimension=0, tiled=True
        ).astype(jnp.float32),
        lax.psum_scatter(
            grad_dec_down.astype(jnp.bfloat16), "dp", scatter_dimension=0, tiled=True
        ).astype(jnp.float32),
    )
    (
        grad_enc_norms,
        grad_enc_qkv,
        grad_enc_proj,
        grad_enc_up,
        grad_enc_down,
        grad_dec_norms,
        grad_dec_qkv,
        grad_dec_self_proj,
        grad_dec_cross_q,
        grad_dec_cross_kv,
        grad_dec_cross_proj,
        grad_dec_up,
        grad_dec_down,
    ) = (
        lax.psum(grad_enc_norms.astype(jnp.bfloat16), "gen").astype(jnp.float32),
        lax.psum(grad_enc_qkv.astype(jnp.bfloat16), "gen").astype(jnp.float32),
        lax.psum(grad_enc_proj.astype(jnp.bfloat16), "gen").astype(jnp.float32),
        lax.psum(grad_enc_up.astype(jnp.bfloat16), "gen").astype(jnp.float32),
        lax.psum(grad_enc_down.astype(jnp.bfloat16), "gen").astype(jnp.float32),
        lax.psum(grad_dec_norms.astype(jnp.bfloat16), "gen").astype(jnp.float32),
        lax.psum(grad_dec_qkv.astype(jnp.bfloat16), "gen").astype(jnp.float32),
        lax.psum(grad_dec_self_proj.astype(jnp.bfloat16), "gen").astype(jnp.float32),
        lax.psum(grad_dec_cross_q.astype(jnp.bfloat16), "gen").astype(jnp.float32),
        lax.psum(grad_dec_cross_kv.astype(jnp.bfloat16), "gen").astype(jnp.float32),
        lax.psum(grad_dec_cross_proj.astype(jnp.bfloat16), "gen").astype(jnp.float32),
        lax.psum(grad_dec_up.astype(jnp.bfloat16), "gen").astype(jnp.float32),
        lax.psum(grad_dec_down.astype(jnp.bfloat16), "gen").astype(jnp.float32),
    )
    return (
        decoded.reshape(row_count, length, model_width).astype(jnp.bfloat16),
        grad_enc_rows.reshape(row_count, length, model_width).astype(jnp.bfloat16),
        grad_dec_rows.reshape(row_count, length, model_width).astype(jnp.bfloat16),
        grad_enc_norms,
        grad_enc_qkv,
        grad_enc_proj,
        grad_enc_up,
        grad_enc_down,
        grad_dec_norms,
        grad_dec_qkv,
        grad_dec_self_proj,
        grad_dec_cross_q,
        grad_dec_cross_kv,
        grad_dec_cross_proj,
        grad_dec_up,
        grad_dec_down,
        grad_task_emb,
        grad_layer_emb,
        grad_proj_task,
        grad_gen_weight,
        grad_gen_vector,
    )


def solution(mesh):
    in_specs = (
        P(("dp", "gen"), None, None),
        P(("dp", "gen"), None, None),
        P(("dp", "gen"), None),
        P(("dp", "gen"), None),
        P(("dp", "gen")),
        P(("dp", "gen"), None, None),
        P(),
        P(),
        P(),
        P(),
        P(),
        P(),
        P(),
        P(),
        P(),
        P(),
        P(),
        P(),
        P(),
        P(),
        P(),
        P(),
        P(None, None, "gen"),
        P(None, None, "gen"),
    )
    out_specs = (
        P(("dp", "gen"), None, None),
        P(("dp", "gen"), None, None),
        P(("dp", "gen"), None, None),
        P(None, "dp"),
        P("dp", None),
        P("dp", None),
        P("dp", None),
        P("dp", None),
        P(None, "dp"),
        P("dp", None),
        P("dp", None),
        P("dp", None),
        P("dp", None),
        P("dp", None),
        P("dp", None),
        P("dp", None),
        P(),
        P(),
        P(),
        P(None, None, "gen"),
        P(None, None, "gen"),
    )
    return jax.shard_map(body, mesh=mesh, in_specs=in_specs, out_specs=out_specs, check_vma=False)
```

profile of v0, /device:TPU:0, one launch (start us, length us, event | category | flops | bytes accessed | tf_op | source)
XLA Modules:
  0.0 1198.4 jit_solution(16772614026253583939)
XLA Ops:
  9.1 3.8 convolution_convert_fusion.19
  12.8 2.9 copy.168
  29.5 34.3 %all_gather.6 = bf16[16,3,768]{0,1,2:T(4,128)(2,1)} all-gather(bf16[16,3,192]{0,1,2:T(4,128)(2,1)} %copy.167), channel_id=1, replica_groups=mesh['dp'=8,'gen'=4] {'gen'}, dimensions={2}, use_global_device_ids=true | all-gather | bytes 92160 | tf_op jit(solution)/shard_map/all_gather | solution.py:270
  69.1 4.4 convolution_convert_fusion.7
  81.8 3.2 convolution_convert_fusion.6
  94.6 3.7 fusion.31
  102.8 6.3 fusion
  109.1 3.6 fusion.66
  118.9 8.5 fusion.65
  129.0 19.9 %multiply_convert_fusion.4 = (bf16[512,3072]{1,0:T(8,128)(2,1)S(1)}, f32[512,3072]{1,0:T(8,128)}, f32[512,3072]{1,0:T(8,128)}) fusion(bf16[768,3072]{1,0:T(8,128)(2,1)} %param.33, f32[512,768]{1,0:T(8,128)S(1)} %get-tuple-element.255, f32[768]{0:T(1024)S(1)} %copy-done.114, f32[512]{0:T(512)S(1)} %fusion.175), kind=kOutput, calls=%fused_computation.49 | convolution fusion | flops 2519334912 | bytes 22025216 | tf_op jit(solution)/shard_map/dot_general | solution.py:14
  154.5 6.1 copy.190
  173.8 3.5 fusion.32
  177.3 3.7 fusion.2
  181.9 4.9 fusion.64
  187.8 20.0 %multiply_convert_fusion.3 = (bf16[512,3072]{1,0:T(8,128)(2,1)S(1)}, f32[512,3072]{1,0:T(8,128)}, f32[512,3072]{1,0:T(8,128)}) fusion(bf16[768,3072]{1,0:T(8,128)(2,1)} %param.41, f32[512,768]{1,0:T(8,128)S(1)} %get-tuple-element.266, f32[768]{0:T(1024)S(1)} %copy-done.120, f32[512]{0:T(512)S(1)} %fusion.179), kind=kOutput, calls=%fused_computation.36 | convolution fusion | flops 2519334912 | bytes 22025216 | tf_op jit(solution)/shard_map/dot_general | solution.py:14
  217.1 8.0 add_convert_fusion.1
  225.1 3.4 multiply_reduce_fusion.6
  234.3 8.1 fusion.55
  242.4 9.7 multiply_reduce_fusion.2
  252.1 7.2 multiply_convert_fusion.2
  280.9 10.9 copy.208
  291.8 12.0 reshape.975
  303.8 3.5 convolution_convert_fusion.11
  308.6 4.5 multiply_convert_fusion.7
  316.3 3.7 fusion.225
  328.1 8.7 add_convert_fusion
  336.9 6.9 multiply_reduce_fusion.8
  348.7 3.5 convolution_convert_fusion.16
  354.5 5.1 convolution_convert_fusion.8
  360.1 13.7 %multiply_reduce_fusion.1 = (f32[12,512]{1,0:T(8,128)S(1)}, f32[12,512,512]{1,2,0:T(8,128)}) fusion(f32[12,512]{1,0:T(8,128)} %log_add_fusion.1, f32[12,512,512]{1,2,0:T(8,128)} %copy-done.2, pred[512,512]{0,1:T(8,128)(4,1)} %copy-done.34, bf16[512,12,64]{0,2,1:T(8,128)(2,1)} %bitcast.348, bf16[512,12,64]{0,2,1:T(8,128)(2,1)} %bitcast.345), kind=kOutput, calls=%fused_computation.4 | convolution fusion | flops 418375680 | bytes 27049984 | tf_op jit(solution)/shard_map/while/body/eval_jaxpr/qhd,khd->hqk/dot_general | solution.py:88
  373.8 7.1 multiply_convert_fusion.1
  380.9 2.9 multiply_convert_fusion.8
  385.0 3.2 fusion.58
  389.1 4.1 convolution_convert_fusion.5
  394.8 3.5 convolution_convert_fusion.15
  400.7 13.7 %multiply_reduce_fusion = (f32[12,512]{1,0:T(8,128)S(1)}, f32[12,512,512]{1,2,0:T(8,128)}) fusion(f32[12,512]{1,0:T(8,128)} %log_add_fusion, f32[12,512,512]{1,2,0:T(8,128)} %copy-done.1, pred[512,512]{0,1:T(8,128)(4,1)} %copy-done.32, bf16[512,12,64]{0,2,1:T(8,128)(2,1)} %bitcast.350, bf16[512,12,64]{0,2,1:T(8,128)(2,1)} %bitcast.342), kind=kOutput, calls=%fused_computation.1 | convolution fusion | flops 418375680 | bytes 27049984 | tf_op jit(solution)/shard_map/while/body/eval_jaxpr/qhd,khd->hqk/dot_general | solution.py:88
  414.4 7.1 multiply_convert_fusion
  421.5 2.9 multiply_convert_fusion.5
  425.6 3.2 fusion.61
  429.7 4.1 convolution_convert_fusion.2
  434.0 6.9 convolution_convert_fusion
  441.6 7.3 convolution_convert_fusion.1
  449.0 7.0 convolution_convert_fusion.3
  456.7 7.3 convolution_convert_fusion.4
  467.7 5.9 fusion.40
  474.5 6.8 fusion.42
  489.9 3.7 reshape.976
  493.6 3.1 copy.209
  496.7 3.5 convolution_convert_fusion.10
  500.4 40.0 %reduce-scatter.38.cloned.1.call-done = bf16[96,1536]{1,0:T(8,128)(2,1)} async-done(((bf16[768,1536]{1,0:T(8,128)(2,1)}), bf16[96,1536]{1,0:T(8,128)(2,1)}) %reduce-scatter.38.cloned.1.call-update) | async-done | bytes 294928 | tf_op jit(solution)/shard_map/reduce_scatter | solution.py:452
  540.4 51.6 %reduce-scatter.24.cloned.1.call-done = bf16[96,2304]{1,0:T(8,128)(2,1)} async-done(((bf16[768,2304]{1,0:T(8,128)(2,1)}), bf16[96,2304]{1,0:T(8,128)(2,1)}) %reduce-scatter.24.cloned.1.call-update) | async-done | bytes 442384 | tf_op jit(solution)/shard_map/reduce_scatter | solution.py:428
  592.0 51.4 %reduce-scatter.32.cloned.1.call-done = bf16[96,2304]{1,0:T(8,128)(2,1)} async-done(((bf16[768,2304]{1,0:T(8,128)(2,1)}), bf16[96,2304]{1,0:T(8,128)(2,1)}) %reduce-scatter.32.cloned.1.call-update) | async-done | bytes 442384 | tf_op jit(solution)/shard_map/reduce_scatter | solution.py:443
  643.4 57.4 %reduce-scatter.44.cloned.1.call-done = bf16[384,768]{1,0:T(8,128)(2,1)} async-done(((bf16[3072,768]{1,0:T(8,128)(2,1)}), bf16[384,768]{1,0:T(8,128)(2,1)}) %reduce-scatter.44.cloned.1.call-update) | async-done | bytes 589840 | tf_op jit(solution)/shard_map/reduce_scatter | solution.py:461
  700.8 57.6 %reduce-scatter.42.cloned.1.call-done = bf16[96,3072]{1,0:T(8,128)(2,1)} async-done(((bf16[768,3072]{1,0:T(8,128)(2,1)}), bf16[96,3072]{1,0:T(8,128)(2,1)}) %reduce-scatter.42.cloned.1.call-update) | async-done | bytes 589840 | tf_op jit(solution)/shard_map/reduce_scatter | solution.py:458
  758.4 57.4 %reduce-scatter.30.cloned.1.call-done = bf16[384,768]{1,0:T(8,128)(2,1)} async-done(((bf16[3072,768]{1,0:T(8,128)(2,1)}), bf16[384,768]{1,0:T(8,128)(2,1)}) %reduce-scatter.30.cloned.1.call-update) | async-done | bytes 589840 | tf_op jit(solution)/shard_map/reduce_scatter | solution.py:437
  815.8 58.2 %reduce-scatter.28.cloned.1.call-done = bf16[96,3072]{1,0:T(8,128)(2,1)} async-done(((bf16[768,3072]{1,0:T(8,128)(2,1)}), bf16[96,3072]{1,0:T(8,128)(2,1)}) %reduce-scatter.28.cloned.1.call-update) | async-done | bytes 589840 | tf_op jit(solution)/shard_map/reduce_scatter | solution.py:434
  875.9 3.3 fusion.67
  882.9 28.0 %reduce-scatter.46.cloned.1.call-done = bf16[96,2]{1,0:T(8,128)(2,1)} async-done(((bf16[768,2]{1,0:T(8,128)(2,1)}), bf16[96,2]{1,0:T(8,128)(2,1)}) %reduce-scatter.46.cloned.1.call-update) | async-done | bytes 400
  912.3 35.9 %reduce-scatter.48.cloned.1.call-done = bf16[96,4]{1,0:T(8,128)(2,1)} async-done(((bf16[768,4]{1,0:T(8,128)(2,1)}), bf16[96,4]{1,0:T(8,128)(2,1)}) %reduce-scatter.48.cloned.1.call-update) | async-done | bytes 784
  949.0 12.3 %all-reduce.1 = (bf16[2,96]{1,0:T(2,128)(2,1)}, bf16[4,96]{1,0:T(4,128)(2,1)S(1)}) all-reduce(bf16[2,96]{1,0:T(2,128)(2,1)} %copy.205, bf16[4,96]{1,0:T(4,128)(2,1)S(1)} %copy.207), channel_id=1, replica_groups=mesh['dp'=8,'gen'=4] {'gen'}, use_global_device_ids=true, to_apply=%region_32.33 | all-reduce | flops 576 | bytes 2304 | tf_op jit(solution)/shard_map/psum | solution.py:480
  967.2 37.4 %psum.125 = f32[8,2,128]{2,0,1:T(8,128)S(1)} all-reduce(f32[8,2,128]{2,0,1:T(8,128)} %copy.185), channel_id=1, replica_groups=mesh['dp'=8,'gen'=4] {'dp','gen'}, use_global_device_ids=true, to_apply=%region_69.70 | all-reduce | flops 2048 | bytes 16384 | tf_op jit(solution)/shard_map/psum | solution.py:408
  1008.2 8.2 all-reduce.6.cloned.1.call-done
  1018.1 4.4 convert_element_type.438
  1022.5 153.7 %all-reduce.8.cloned.1.call-done = (bf16[96,2304]{1,0:T(8,128)(2,1)}, bf16[96,768]{1,0:T(8,128)(2,1)}, bf16[96,3072]{1,0:T(8,128)(2,1)}, bf16[384,768]{1,0:T(8,1...) async-done(((bf16[96,2304]{1,0:T(8,128)(2,1)}, ...) | async-done | bytes 4128784 | tf_op jit(solution)/shard_map/psum | solution.py:481
  (560 shorter events, 183.8 us)
Async XLA Ops:
  7.2 74.6 %copy-start = (bf16[768,2304]{1,0:T(8,128)(2,1)S(1)}, bf16[768,2304]{1,0:T(8,128)(2,1)}, u32[]{:S(2)}) copy-start(bf16[768,2304]{1,0:T(8,128)(2,1)} %param.31) | copy-start | bytes 10616836
  7.2 147.3 %all-gather.2.cloned.1.call-start = ((), (), s32[]{:S(2)}) async-start(), calls=%async_computation.15 | async-start | bytes 3932160 | tf_op jit(solution)/shard_map/all_gather | solution.py:269
  9.0 17.2 %copy-start.89 = (f32[8,2,128]{2,1,0:T(2,128)}, f32[8,2,128]{2,1,0:T(2,128)S(1)}, u32[]{:S(2)}) copy-start(f32[8,2,128]{2,1,0:T(2,128)S(1)} %copy.166) | copy-start | bytes 24580
  9.0 17.2 %copy-start.91 = (f32[8,2,128]{2,1,0:T(2,128)}, f32[8,2,128]{2,1,0:T(2,128)S(1)}, u32[]{:S(2)}) copy-start(f32[8,2,128]{2,1,0:T(2,128)S(1)} %copy.165) | copy-start | bytes 24580
  15.7 469.3 %reduce-scatter.52.cloned.1.call-start = ((), (), s32[]{:S(2)}) async-start(), calls=%async_computation.30 | async-start | bytes 245760
  94.6 14.5 %copy-start.32 = (pred[512,512]{0,1:T(8,128)(4,1)}, pred[512,512]{0,1:T(8,128)(4,1)S(1)}, u32[]{:S(2)}) copy-start(pred[512,512]{0,1:T(8,128)(4,1)S(1)} %get-tuple-element.249) | copy-start | bytes 786436
  100.4 8.7 copy-start.1
  100.4 8.7 copy-start.81
  118.9 8.5 copy-start.154
  127.4 21.5 %copy-start.62 = (bf16[12,64,512]{2,1,0:T(8,128)(2,1)}, bf16[12,64,512]{2,1,0:T(8,128)(2,1)S(1)}, u32[]{:S(2)}) copy-start(bf16[12,64,512]{2,1,0:T(8,128)(2,1)S(1)} %fusion.65) | copy-start | bytes 2359300
  127.4 22.0 %slice-start.15 = ((s8[4718592]{0:T(1024)(128)(4,1)}), s8[4194304]{0:T(1024)(128)(4,1)S(1)}, s32[]{:S(2)}) async-start(s8[4718592]{0:T(1024)(128)(4,1)} %bitcast.393), calls=%async_computation.48 | async-start | bytes 8388608
  128.4 20.5 %copy-start.39 = (f32[512,768]{1,0:T(8,128)}, f32[512,768]{1,0:T(8,128)S(1)}, u32[]{:S(2)}) copy-start(f32[512,768]{1,0:T(8,128)S(1)} %get-tuple-element.255) | copy-start | bytes 4718596
  128.9 19.9 %copy-start.134 = (f32[512]{0:T(512)}, f32[512]{0:T(512)S(1)}, u32[]{:S(2)}) copy-start(f32[512]{0:T(512)S(1)} %fusion.175) | copy-start | bytes 6148
  128.9 20.5 %slice-start.16 = ((s8[4718592]{0:T(1024)(128)(4,1)}), s8[524288]{0:T(1024)(128)(4,1)S(1)}, s32[]{:S(2)}) async-start(s8[4718592]{0:T(1024)(128)(4,1)} %bitcast.393), calls=%async_computation.49 | async-start | bytes 1048576
  181.9 25.9 %slice-start.9 = ((s8[4718592]{0:T(1024)(128)(4,1)}), s8[524288]{0:T(1024)(128)(4,1)S(1)}, s32[]{:S(2)}) async-start(s8[4718592]{0:T(1024)(128)(4,1)} %bitcast.387), calls=%async_computation.42 | async-start | bytes 1048576
  186.8 21.0 %copy-start.49 = (bf16[12,64,512]{2,1,0:T(8,128)(2,1)}, bf16[12,64,512]{2,1,0:T(8,128)(2,1)S(1)}, u32[]{:S(2)}) copy-start(bf16[12,64,512]{2,1,0:T(8,128)(2,1)S(1)} %fusion.64) | copy-start | bytes 2359300
  187.8 40.7 %copy-start.17 = (f32[512,768]{1,0:T(8,128)}, f32[512,768]{1,0:T(8,128)S(1)}, u32[]{:S(2)}) copy-start(f32[512,768]{1,0:T(8,128)S(1)} %get-tuple-element.266) | copy-start | bytes 4718596
  187.8 40.7 %copy-start.137 = (f32[512]{0:T(512)}, f32[512]{0:T(512)S(1)}, u32[]{:S(2)}) copy-start(f32[512]{0:T(512)S(1)} %fusion.179) | copy-start | bytes 6148
  187.8 20.0 %slice-start.10 = ((s8[4718592]{0:T(1024)(128)(4,1)}), s8[4194304]{0:T(1024)(128)(4,1)S(1)}, s32[]{:S(2)}) async-start(s8[4718592]{0:T(1024)(128)(4,1)} %bitcast.387), calls=%async_computation.43 | async-start | bytes 8388608
  215.8 9.3 slice-start.13
  234.2 17.9 %slice-start.6 = ((s8[12582912]{0:T(1024)(128)(4,1)}), s8[4194304]{0:T(1024)(128)(4,1)S(1)}, s32[]{:S(2)}) async-start(s8[12582912]{0:T(1024)(128)(4,1)} %bitcast.324), calls=%async_computation.39 | async-start | bytes 8388608
  234.3 17.9 %slice-start.7 = ((s8[12582912]{0:T(1024)(128)(4,1)}), s8[4194304]{0:T(1024)(128)(4,1)S(1)}, s32[]{:S(2)}) async-start(s8[12582912]{0:T(1024)(128)(4,1)} %bitcast.324), calls=%async_computation.40 | async-start | bytes 8388608
  242.4 20.2 %copy-start.156 = (bf16[12,64,512]{2,1,0:T(8,128)(2,1)}, bf16[12,64,512]{2,1,0:T(8,128)(2,1)S(1)}, u32[]{:S(2)}) copy-start(bf16[12,64,512]{2,1,0:T(8,128)(2,1)S(1)} %fusion.55) | copy-start | bytes 2359300
  242.4 9.7 slice-start.8
  276.9 213.0 %reduce-scatter.50.cloned.1.call-start = ((), (), s32[]{:S(2)}) async-start(), calls=%async_computation.29 | async-start | bytes 1474560
  303.8 196.5 %reduce-scatter.40.cloned.1.call-start = ((), (), s32[]{:S(2)}) async-start(), calls=%async_computation.24 | async-start | bytes 1327104 | tf_op jit(solution)/shard_map/reduce_scatter | solution.py:455
  307.3 193.0 %reduce-scatter.36.cloned.1.call-start = ((), (), s32[]{:S(2)}) async-start(), calls=%async_computation.22 | async-start | bytes 1327104 | tf_op jit(solution)/shard_map/reduce_scatter | solution.py:449
  316.0 184.3 %reduce-scatter.34.cloned.1.call-start = ((), (), s32[]{:S(2)}) async-start(), calls=%async_computation.21 | async-start | bytes 1327104 | tf_op jit(solution)/shard_map/reduce_scatter | solution.py:446
  325.9 174.4 %reduce-scatter.26.cloned.1.call-start = ((), (), s32[]{:S(2)}) async-start(), calls=%async_computation.17 | async-start | bytes 1327104 | tf_op jit(solution)/shard_map/reduce_scatter | solution.py:431
  328.1 8.7 copy-start.66
  328.1 8.7 copy-start.41
  328.1 8.7 copy-start.115
  328.1 8.7 copy-start.135
  347.2 193.1 %reduce-scatter.38.cloned.1.call-start = ((), (), s32[]{:S(2)}) async-start(), calls=%async_computation.23 | async-start | bytes 2654208 | tf_op jit(solution)/shard_map/reduce_scatter | solution.py:452
  359.5 232.5 %reduce-scatter.24.cloned.1.call-start = ((), (), s32[]{:S(2)}) async-start(), calls=%async_computation.16 | async-start | bytes 3981312 | tf_op jit(solution)/shard_map/reduce_scatter | solution.py:428
  360.0 13.8 %slice-start.3 = ((s8[12582912]{0:T(1024)(128)(4,1)}), s8[4194304]{0:T(1024)(128)(4,1)S(1)}, s32[]{:S(2)}) async-start(s8[12582912]{0:T(1024)(128)(4,1)} %bitcast.322), calls=%async_computation.36 | async-start | bytes 8388608
  360.0 13.8 %slice-start.4 = ((s8[12582912]{0:T(1024)(128)(4,1)}), s8[4194304]{0:T(1024)(128)(4,1)S(1)}, s32[]{:S(2)}) async-start(s8[12582912]{0:T(1024)(128)(4,1)} %bitcast.322), calls=%async_computation.37 | async-start | bytes 8388608
  360.0 13.7 %slice-start.5 = ((s8[12582912]{0:T(1024)(128)(4,1)}), s8[4194304]{0:T(1024)(128)(4,1)S(1)}, s32[]{:S(2)}) async-start(s8[12582912]{0:T(1024)(128)(4,1)} %bitcast.322), calls=%async_computation.38 | async-start | bytes 8388608
  360.0 13.7 %copy-start.35 = (pred[512,512]{0,1:T(8,128)(4,1)S(1)}, pred[512,512]{0,1:T(8,128)(4,1)}, u32[]{:S(2)}) copy-start(pred[512,512]{0,1:T(8,128)(4,1)} %copy-done.34) | copy-start | bytes 786436
  360.0 13.7 %copy-start.85 = (f32[12,512]{1,0:T(8,128)S(1)}, f32[12,512]{1,0:T(8,128)}, u32[]{:S(2)}) copy-start(f32[12,512]{1,0:T(8,128)} %log_add_fusion.1) | copy-start | bytes 73732
  393.2 250.3 %reduce-scatter.32.cloned.1.call-start = ((), (), s32[]{:S(2)}) async-start(), calls=%async_computation.20 | async-start | bytes 3981312 | tf_op jit(solution)/shard_map/reduce_scatter | solution.py:443
  400.7 13.7 %slice-start = ((s8[12582912]{0:T(1024)(128)(4,1)}), s8[4194304]{0:T(1024)(128)(4,1)S(1)}, s32[]{:S(2)}) async-start(s8[12582912]{0:T(1024)(128)(4,1)} %bitcast.320), calls=%async_computation.33 | async-start | bytes 8388608
  400.7 13.7 %slice-start.1 = ((s8[12582912]{0:T(1024)(128)(4,1)}), s8[4194304]{0:T(1024)(128)(4,1)S(1)}, s32[]{:S(2)}) async-start(s8[12582912]{0:T(1024)(128)(4,1)} %bitcast.320), calls=%async_computation.34 | async-start | bytes 8388608
  400.7 13.7 %slice-start.2 = ((s8[12582912]{0:T(1024)(128)(4,1)}), s8[4194304]{0:T(1024)(128)(4,1)S(1)}, s32[]{:S(2)}) async-start(s8[12582912]{0:T(1024)(128)(4,1)} %bitcast.320), calls=%async_computation.35 | async-start | bytes 8388608
  400.7 13.7 %copy-start.33 = (pred[512,512]{0,1:T(8,128)(4,1)S(1)}, pred[512,512]{0,1:T(8,128)(4,1)}, u32[]{:S(2)}) copy-start(pred[512,512]{0,1:T(8,128)(4,1)} %copy-done.32) | copy-start | bytes 786436
  400.7 13.7 %copy-start.86 = (f32[12,512]{1,0:T(8,128)S(1)}, f32[12,512]{1,0:T(8,128)}, u32[]{:S(2)}) copy-start(f32[12,512]{1,0:T(8,128)} %log_add_fusion) | copy-start | bytes 73732
  433.7 267.0 %reduce-scatter.44.cloned.1.call-start = ((), (), s32[]{:S(2)}) async-start(), calls=%async_computation.26 | async-start | bytes 5308416 | tf_op jit(solution)/shard_map/reduce_scatter | solution.py:461
  440.9 317.5 %reduce-scatter.42.cloned.1.call-start = ((), (), s32[]{:S(2)}) async-start(), calls=%async_computation.25 | async-start | bytes 5308416 | tf_op jit(solution)/shard_map/reduce_scatter | solution.py:458
  449.0 366.8 %reduce-scatter.30.cloned.1.call-start = ((), (), s32[]{:S(2)}) async-start(), calls=%async_computation.19 | async-start | bytes 5308416 | tf_op jit(solution)/shard_map/reduce_scatter | solution.py:437
  456.0 417.9 %reduce-scatter.28.cloned.1.call-start = ((), (), s32[]{:S(2)}) async-start(), calls=%async_computation.18 | async-start | bytes 5308416 | tf_op jit(solution)/shard_map/reduce_scatter | solution.py:434
  464.0 447.0 %reduce-scatter.46.cloned.1.call-start = ((), (), s32[]{:S(2)}) async-start(), calls=%async_computation.27 | async-start | bytes 221184
  474.5 13.7 %copy-start.90 = (f32[8,2,128]{2,1,0:T(2,128)S(1)}, f32[8,2,128]{2,1,0:T(2,128)}, u32[]{:S(2)}) copy-start(f32[8,2,128]{2,1,0:T(2,128)} %copy-done.89) | copy-start | bytes 24580
  474.5 13.7 %copy-start.92 = (f32[8,2,128]{2,1,0:T(2,128)S(1)}, f32[8,2,128]{2,1,0:T(2,128)}, u32[]{:S(2)}) copy-start(f32[8,2,128]{2,1,0:T(2,128)} %copy-done.91) | copy-start | bytes 24580
  481.9 466.3 %reduce-scatter.48.cloned.1.call-start = ((), (), s32[]{:S(2)}) async-start(), calls=%async_computation.28 | async-start | bytes 221184
  484.9 531.5 %all-reduce.6.cloned.1.call-start = ((), (), s32[]{:S(2)}) async-start(), calls=%async_computation.31 | async-start | bytes 5013504 | tf_op jit(solution)/shard_map/psum | solution.py:405
  500.2 373.8 %copy-start.104 = (f32[512]{0:T(512)S(1)}, f32[512]{0:T(512)}, u32[]{:S(2)}) copy-start(f32[512]{0:T(512)} %copy-done.103) | copy-start | bytes 6148
  500.2 374.7 %copy-start.102 = (f32[512]{0:T(512)S(1)}, f32[512]{0:T(512)}, u32[]{:S(2)}) copy-start(f32[512]{0:T(512)} %copy-done.101) | copy-start | bytes 6148
  500.2 375.7 %copy-start.125 = (f32[768]{0:T(1024)S(1)}, f32[768]{0:T(1024)}, u32[]{:S(2)}) copy-start(f32[768]{0:T(1024)} %get-tuple-element.180) | copy-start | bytes 9220
  500.2 675.9 %all-reduce.8.cloned.1.call-start = ((), (), s32[]{:S(2)}) async-start(), calls=%async_computation.32 | async-start | bytes 8257536 | tf_op jit(solution)/shard_map/psum | solution.py:481
  881.6 123.0 %copy-start.95 = (f32[8,128]{1,0:T(8,128)S(1)}, f32[8,128]{1,0:T(8,128)}, u32[]{:S(2)}) copy-start(f32[8,128]{1,0:T(8,128)} %copy-done.94) | copy-start | bytes 12292
  881.6 125.8 %copy-start.147 = (f32[8,64]{1,0:T(8,128)S(1)}, f32[8,64]{1,0:T(8,128)}, u32[]{:S(2)}) copy-start(f32[8,64]{1,0:T(8,128)} %param.43) | copy-start | bytes 6148
  1176.2 8.7 copy-start.83
  1176.2 9.6 copy-start.80
  1176.2 10.6 copy-start.74
  (134 other events, 490.1 us)
Sparse Core Ops, SparseCore 0:
  15.8 78.6 all-gather.1
  277.0 19.1 reduce-scatter.51
  303.9 28.9 reduce-scatter.49
  336.8 35.4 reduce-scatter.39
  376.0 36.7 reduce-scatter.35
  416.8 36.7 reduce-scatter.33
  457.4 36.7 reduce-scatter.25
  497.9 42.4 reduce-scatter.37
  543.9 48.0 reduce-scatter.23
  595.3 48.0 reduce-scatter.31
  646.9 53.8 reduce-scatter.43
  704.5 53.8 reduce-scatter.41
  761.8 53.8 reduce-scatter.29
  820.0 53.8 reduce-scatter.27
  877.4 33.5 reduce-scatter.45
  914.7 33.4 reduce-scatter.47
  952.0 64.3 all-reduce.5
  1020.0 156.1 all-reduce.7
where the time goes:
time: 1200 us
  waiting for transfers between devices  600 us (50%)
  matrix products  291 us (24%)
  local copies, waits for them, and re-layouts  111 us (9%)
  other arithmetic  93.1 us (8%)
  blocking collectives  84 us (7%)
  between operations  17.5 us (1%)
    psum x1, waiting for transfers between devices, body(): lax.psum(grad_enc_qkv.astype(jnp.bfloat16), 'gen').astype(jnp.float32)  154 us
    unnamed x22, waiting for transfers between devices  64.3 us
    unnamed x372, local copies, waits for them, and re-layouts  61.3 us
    dot_general x11, matrix products, product(): return jnp.dot(left_side, right_side, preferred_element_type=jnp.float32)  58.8 us
    reduce_scatter x1, waiting for transfers between devices, body(): lax.psum_scatter(grad_enc_up.astype(jnp.bfloat16), 'dp', scatter_dimensio...  58.2 us
    reduce_scatter x1, waiting for transfers between devices, body(): lax.psum_scatter(grad_dec_up.astype(jnp.bfloat16), 'dp', scatter_dimensio...  57.6 us
    reduce_scatter x1, waiting for transfers between devices, body(): lax.psum_scatter(grad_enc_down.astype(jnp.bfloat16), 'dp', scatter_dimens...  57.4 us
    reduce_scatter x1, waiting for transfers between devices, body(): lax.psum_scatter(grad_dec_down.astype(jnp.bfloat16), 'dp', scatter_dimens...  57.4 us
  transfers between devices with their start and end apart: 18, of which 11 were waited for; matrix products, arithmetic and copies ran while one was open for 28% of the time, Pallas kernels for 0%

commit v1 on v0

v1 whole, which is shorter than its diff:
```python
import functools
from typing import NamedTuple

import jax
import jax.numpy as jnp
from jax import lax
from jax.experimental import pallas as pl
from jax.experimental.pallas import tpu as pltpu
from jax.sharding import PartitionSpec as P

H = 12
HD = 64
GROUP = 4 * HD
WIDE_GROUP = 6 * HD
VMEM_LIMIT = 60 * 1024 * 1024
LAGS = (2, 2, 2, 2)
HIGHEST = lax.Precision.HIGHEST
LOW = jnp.bfloat16
WIDE = jnp.float32


def dot_nn(left_side, right_side):
    return jnp.dot(left_side, right_side, preferred_element_type=WIDE)


def dot_nt(left_side, right_side):
    return lax.dot_general(
        left_side, right_side, (((1,), (1,)), ((), ())), preferred_element_type=WIDE
    )


def gelu_parts(values):
    size = jnp.abs(values)
    density = jnp.exp(values * values * -0.5) * 0.3989422804014327
    bottom = 1.0 + 0.2316419 * size
    inverse = pl.reciprocal(bottom, approx=True)
    inverse = inverse * (2.0 - bottom * inverse)
    series = 1.330274429 * inverse - 1.821255978
    series = series * inverse + 1.781477937
    series = series * inverse - 0.356563782
    series = series * inverse + 0.31938153
    tail = series * inverse * density
    return jnp.where(values < 0.0, tail, 1.0 - tail), density


def rms_scale(values):
    return lax.rsqrt(jnp.mean(values * values, axis=-1, keepdims=True) + 1e-06)


def rms_backward(values, norm_gain, grad):
    scale = rms_scale(values)
    normed = values * scale
    pulled = grad * norm_gain
    inner = jnp.mean(normed * pulled, axis=-1, keepdims=True)
    grad_values = scale * (pulled - normed * inner)
    return grad_values, jnp.sum(grad * normed, axis=0, keepdims=True)


def segment_bias(seg_query, seg_key, causal):
    length = seg_query.shape[1]
    column = jnp.broadcast_to(seg_query.astype(WIDE), (128, length)).T[:, :1]
    allowed = column == seg_key.astype(WIDE)
    if causal:
        query_place = lax.broadcasted_iota(jnp.int32, (length, length), 0)
        key_place = lax.broadcasted_iota(jnp.int32, (length, length), 1)
        allowed = allowed & (query_place >= key_place)
    return jnp.where(allowed, 0.0, -1e30)


def row_of(ref, row):
    return ref[row : row + 1].astype(WIDE)


def first_half(shape):
    return lax.broadcasted_iota(jnp.int32, shape, 1) < HD


class Attended(NamedTuple):
    x_t: object
    memory_t: object
    q_t: object
    keys: object
    values: object
    mixed_t: object
    probs: object


class Fed(NamedTuple):
    ffn: object
    x_t: object
    active_t: object
    slope: object


class Gather:
    def __init__(self, n_gen, bottleneck, refs):
        self.n_gen, self.bottleneck, self.line = n_gen, bottleneck, lax.axis_index("gen")
        (
            self.weights, self.pieces, self.more, self.adapters, self.vectors,
            self.asked, self.chosen, self.arrived, self.sems,
        ) = refs

    @staticmethod
    def scratch(n_gen, features):
        return (
            pltpu.VMEM((n_gen, 8, 128), WIDE),
            pltpu.VMEM((n_gen, 2, 64, features), LOW),
            pltpu.VMEM((n_gen, 2, 64, features), LOW),
            pltpu.SemaphoreType.DMA((4, max(n_gen - 1, 1))),
        )

    def ask(self, k):
        sems = self.sems
        return gen_copy(
            self.weights, self.asked, sems.at[0], sems.at[1], self.line, k, self.n_gen
        )

    def answer(self, k):
        sems = self.sems
        return gen_copy(
            self.chosen.at[k], self.arrived, sems.at[2], sems.at[3], self.line, k, self.n_gen
        )

    def pick(self, target, weights):
        for layer in range(2):
            start = 0
            for source in (self.pieces, self.more):
                pairs, rows, features = source.shape
                total = jnp.zeros((rows, features), WIDE)
                for pair in range(pairs):
                    weight = weights[layer : layer + 1, pair : pair + 1]
                    total = total + weight * source[pair].astype(WIDE)
                target[layer, start : start + rows] = total.astype(LOW)
                start += rows

    def step(self, step):
        n_gen, size = self.n_gen, self.bottleneck

        @pl.when(step == 0)
        def _():
            if n_gen > 1:
                gen_barrier(self.line, n_gen)
            for k in range(1, n_gen):
                self.ask(k).start()

        @pl.when(step == 1)
        def _():
            for k in range(1, n_gen):
                self.ask(k).wait()
            for k in range(1, n_gen):
                self.pick(self.chosen.at[k], self.asked[(self.line + k) % n_gen])
                self.answer(k).start()
            self.pick(self.arrived.at[self.line], self.weights[...])

    def finish(self):
        n_gen, size = self.n_gen, self.bottleneck

        @pl.when(pl.program_id(0) == pl.num_programs(0) - 1)
        def _():
            for k in range(1, n_gen):
                self.answer(k).wait()
            rows = 2 * size + 3
            self.adapters[...] = jnp.zeros_like(self.adapters)
            for layer in range(2):
                joined = jnp.concatenate(
                    [self.arrived[j, layer, 0:rows].astype(WIDE) for j in range(n_gen)], axis=1
                ).astype(LOW)
                self.adapters[layer, 0, 0:size] = joined[0:size]
                self.adapters[layer, 1, 0:size] = joined[size : 2 * size]
                self.vectors[layer] = joined[2 * size : 2 * size + 3]


def attention_forward_kernel(
    cross, causal, gather, gain_rows,
    x_ref, gain_ref, memory_ref, memory_gain_ref, seg_q_ref, seg_k_ref,
    wq_ref, wk_ref, wv_ref, wo_ref, *refs,
):
    step = pl.program_id(0)
    more_in = refs[:3] if gather else ()
    refs = refs[len(more_in) :]
    hidden_ref, x_t_ref, memory_t_ref, q_t_ref, k_ref, v_ref, mixed_t_ref, probs_ref = refs[:8]
    more_out = refs[8:10] if gather else ()
    refs = refs[8 + len(more_out) :]
    x_low, memory_low, bias = refs[:3]
    if gather:
        work = Gather(*gather, more_in + more_out + refs[3:])
        work.step(step)

    @pl.when(step == 0)
    def _():
        values = x_ref[...].astype(WIDE)
        hidden_ref[...] = values
        normed = (values * rms_scale(values) * row_of(gain_ref, gain_rows[0])).astype(LOW)
        x_low[...] = normed
        x_t_ref[...] = normed.T
        if cross:
            values = memory_ref[...].astype(WIDE)
            normed = (values * rms_scale(values) * row_of(memory_gain_ref, gain_rows[1])).astype(LOW)
            memory_low[...] = normed
            memory_t_ref[...] = normed.T
        bias[...] = segment_bias(seg_q_ref[...], seg_k_ref[...], causal)

    source_low = memory_low if cross else x_low
    queries = dot_nn(x_low[...], wq_ref[...]).astype(LOW)
    q_t_ref[...] = queries.T
    k_ref[...] = dot_nn(source_low[...], wk_ref[...]).astype(LOW)
    v_ref[...] = dot_nn(source_low[...], wv_ref[...]).astype(LOW)
    scaled = queries * LOW(HD ** (-0.5))
    length = scaled.shape[0]
    lanes = first_half((length, 2 * HD))
    heads = range(scaled.shape[1] // HD)

    def pair_of(ref, head):
        pair = head // 2
        return ref[:, pair * 2 * HD : (pair + 1) * 2 * HD]

    scores = []
    for head in heads:
        mine = jnp.where(lanes if head % 2 == 0 else ~lanes, pair_of(scaled, head), LOW(0))
        scores.append(dot_nt(mine, pair_of(k_ref, head)))
    scores = jnp.stack(scores) + bias[...][None]
    raised = jnp.exp(scores - jnp.max(scores, axis=-1, keepdims=True))
    total = jnp.sum(raised, axis=-1, keepdims=True)
    probs = (raised * (1.0 / total)).astype(LOW)
    probs_ref[...] = probs
    halves = [dot_nn(probs[head], pair_of(v_ref, head)) for head in heads]
    parts = [
        jnp.where(lanes, halves[head], halves[head + 1]).astype(LOW) for head in heads[::2]
    ]
    mixed = jnp.concatenate(parts, axis=1)
    mixed_t_ref[...] = mixed.T
    hidden_ref[...] += dot_nn(mixed, wo_ref[...])
    if gather:
        work.finish()


def whole(shape):
    return pl.BlockSpec(shape, lambda *_: (0,) * len(shape))


def attention_forward(
    x, gains, gain_rows, memory, seg_q, seg_k, weights, w_out, causal, gather=None
):
    n_gen = lax.axis_size("gen")
    more_in, more_out, more_scratch, asked = (), (), (), None
    if gather is not None:
        wanted, pieces, more_pieces, bottleneck = gather
        more_in = (wanted, pieces, more_pieces)
        padded = -bottleneck % 16 + bottleneck
        more_out = (
            jax.ShapeDtypeStruct((2, 2, padded, x.shape[1]), LOW),
            jax.ShapeDtypeStruct((2, 3, x.shape[1]), LOW),
        )
        more_scratch = Gather.scratch(n_gen, pieces.shape[2])
        asked = (n_gen, bottleneck)
    remote = gather is not None and n_gen > 1
    cross = memory is not None
    length, width = x.shape
    groups = width // WIDE_GROUP
    if not cross:
        memory = x
    shape = jax.ShapeDtypeStruct
    columns = pl.BlockSpec((length, WIDE_GROUP), lambda g: (0, g))
    rows = pl.BlockSpec((WIDE_GROUP, length), lambda g: (g, 0))

    def weight_spec(offset):
        return pl.BlockSpec((width, WIDE_GROUP), lambda g: (0, offset + g))

    memory_spec = whole((length, width)) if cross else whole((16, 128))
    memory_t_shape = (width, length) if cross else (16, 128)
    outs = pl.pallas_call(
        functools.partial(attention_forward_kernel, cross, causal, asked, gain_rows),
        grid=(groups,),
        in_specs=[
            whole((length, width)),
            whole(gains.shape),
            memory_spec,
            whole(gains.shape),
            whole((1, length)),
            whole((1, length)),
            weight_spec(weights[0][1] * groups),
            weight_spec(weights[1][1] * groups),
            weight_spec(weights[2][1] * groups),
            pl.BlockSpec((WIDE_GROUP, width), lambda g: (g, 0)),
        ]
        + [whole(one.shape) for one in more_in],
        out_specs=[
            whole((length, width)),
            whole((width, length)),
            whole(memory_t_shape),
            rows,
            columns,
            columns,
            rows,
            pl.BlockSpec((6, length, length), lambda g: (g, 0, 0)),
        ]
        + [whole(one.shape) for one in more_out],
        out_shape=[
            shape((length, width), WIDE),
            shape((width, length), LOW),
            shape(memory_t_shape, LOW),
            shape((width, length), LOW),
            shape((length, width), LOW),
            shape((length, width), LOW),
            shape((width, length), LOW),
            shape((H, length, length), LOW),
            *more_out,
        ],
        scratch_shapes=[
            pltpu.VMEM((length, width), LOW),
            pltpu.VMEM((length, width) if cross else (16, 128), LOW),
            pltpu.VMEM((length, length), WIDE),
            *more_scratch,
        ],
        compiler_params=pltpu.CompilerParams(
            vmem_limit_bytes=VMEM_LIMIT,
            **(dict(collective_id=1, has_side_effects=True) if remote else {}),
        ),
        cost_estimate=pl.CostEstimate(
            flops=2 * length * width * (4 * width + 2 * length),
            bytes_accessed=2 * (4 * width * width + H * length * length + 8 * length * width),
            transcendentals=H * length * length,
        ),
        name="attention_forward",
    )(x, gains, memory, gains, seg_q, seg_k,
      weights[0][0], weights[1][0], weights[2][0], w_out, *more_in)
    hidden, x_t, memory_t, q_t, keys, values, mixed_t, probs = outs[:8]
    stored = Attended(x_t, memory_t if cross else None, q_t, keys, values, mixed_t, probs)
    return (hidden, stored) + tuple(outs[8:])


def layer_parts(values):
    centred = values - jnp.mean(values, axis=-1, keepdims=True)
    scale = lax.rsqrt(jnp.mean(centred * centred, axis=-1, keepdims=True) + 1e-05)
    return centred * scale, scale


def feed_forward_kernel(
    up_scale, layer, gain_row,
    x_ref, gain_ref, up_ref, down_ref, adapter_ref, vector_ref,
    out_ref, ffn_ref, x_t_ref, active_t_ref, slope_ref,
    x_low, total,
):
    step = pl.program_id(0)

    @pl.when(step == 0)
    def _():
        values = x_ref[...]
        normed = (values * rms_scale(values) * row_of(gain_ref, gain_row)).astype(LOW)
        x_low[...] = normed
        x_t_ref[...] = normed.T
        total[...] = jnp.zeros_like(total)

    before = dot_nn(x_low[...], up_ref[...])
    cumulative, density = gelu_parts(before)
    active = (before * cumulative).astype(LOW)
    slope_ref[...] = (cumulative + before * density).astype(LOW)
    active_t_ref[...] = active.T
    total[...] += dot_nn(active, down_ref[...])

    @pl.when(step == pl.num_programs(0) - 1)
    def _():
        ffn = total[...]
        ffn_ref[...] = ffn
        normed, _ = layer_parts(ffn)
        vectors = vector_ref[layer].astype(WIDE)
        low = (normed * (1.0 + vectors[1:2]) + vectors[2:3]).astype(LOW)
        inner = dot_nt(low, adapter_ref[layer, 0])
        gate = (inner * gelu_parts(inner)[0]).astype(LOW)
        adapted = dot_nn(gate, adapter_ref[layer, 1]) * up_scale + vectors[0:1]
        out_ref[...] = (x_ref[...] + ffn + adapted).astype(out_ref.dtype)


def feed_forward(
    x, gains, gain_row, w_up, w_down, adapter, vectors, layer, up_scale, out_dtype, blocks=2
):
    length, width = x.shape
    inner = w_up.shape[1]
    block = inner // blocks
    shape = jax.ShapeDtypeStruct
    out, ffn, x_t, active_t, slope = pl.pallas_call(
        functools.partial(feed_forward_kernel, up_scale, layer, gain_row),
        grid=(blocks,),
        in_specs=[
            whole((length, width)),
            whole(gains.shape),
            pl.BlockSpec((width, block), lambda j: (0, j)),
            pl.BlockSpec((block, width), lambda j: (j, 0)),
            whole(adapter.shape),
            whole(vectors.shape),
        ],
        out_specs=[
            whole((length, width)),
            whole((length, width)),
            whole((width, length)),
            pl.BlockSpec((block, length), lambda j: (j, 0)),
            pl.BlockSpec((length, block), lambda j: (0, j)),
        ],
        out_shape=[
            shape((length, width), out_dtype),
            shape((length, width), WIDE),
            shape((width, length), LOW),
            shape((inner, length), LOW),
            shape((length, inner), LOW),
        ],
        scratch_shapes=[pltpu.VMEM((length, width), LOW), pltpu.VMEM((length, width), WIDE)],
        compiler_params=pltpu.CompilerParams(vmem_limit_bytes=VMEM_LIMIT),
        cost_estimate=pl.CostEstimate(
            flops=4 * length * width * inner,
            bytes_accessed=4 * width * inner + 4 * length * inner + 12 * length * width,
            transcendentals=length * inner,
        ),
        name="feed_forward",
    )(x, gains, w_up, w_down, adapter, vectors)
    return out, Fed(ffn, x_t, active_t, slope)


def join_rows(ref):
    blocks, _, rows, columns = ref.shape
    if rows % 16 == 0:
        return ref[...].reshape(blocks * rows, columns)
    parts = [ref[i, 0].astype(WIDE) for i in range(blocks)]
    return jnp.concatenate(parts, axis=0).astype(LOW)


def power_of_two(least):
    return 1 << (least - 1).bit_length()


class TransferRefs(NamedTuple):
    unit: object
    held: object
    into: object
    total: object
    line: object
    send: object
    recv: object


class Transfer:
    def __init__(self, units, small, n_dp, n_gen, rows, width, lags):
        self.units, self.small, self.n_dp, self.n_gen = units, small, n_dp, n_gen
        self.rows, self.width = rows, width
        self.bits = n_dp.bit_length() - 1
        self.final = self.bits + max(n_gen - 1, 0)
        first, between, last, along = lags
        self.lags = [first] + [between] * (self.bits - 2) + [last] + [along] * (n_gen - 1)
        self.at = [sum(self.lags[:s]) for s in range(self.final + 1)]
        self.slots = units + self.at[self.final]
        self.ring = power_of_two(2 * max(first, between, last) + 1)
        self.line_ring = power_of_two(max(2 * along + 1, along * (n_gen - 1)))
        self.unit_ring = power_of_two(first + 1)
        self.sum_ring = power_of_two(along * max(n_gen - 1, 1) + 1)

    def scratch(self):
        block = (self.rows, self.width)
        bits, lags, ring = self.bits, self.lags, self.ring
        stages = max(bits + self.n_gen - 1, 1)
        return TransferRefs(
            unit=pltpu.VMEM((self.unit_ring, self.n_dp) + block, LOW),
            held=[pltpu.VMEM((lags[s], self.n_dp >> s) + block, LOW) for s in range(1, bits)],
            into=[pltpu.VMEM((ring, self.n_dp >> (s + 1)) + block, LOW) for s in range(bits)],
            total=pltpu.VMEM((self.sum_ring,) + block, LOW),
            line=[pltpu.VMEM((self.line_ring,) + block, LOW) for _ in range(self.n_gen - 1)],
            send=pltpu.SemaphoreType.DMA((stages, max(ring, self.line_ring))),
            recv=pltpu.SemaphoreType.DMA((stages, max(ring, self.line_ring))),
        )

    def bind(self, refs):
        self.refs = refs
        self.place = lax.axis_index("dp")
        self.at_line = lax.axis_index("gen")
        self.core = self.place % 2
        self.partners = [self.partner(step) for step in range(self.bits)]
        self.positions = [self.position(index) for index in range(self.n_dp)]

    def partner(self, step):
        if step == 0:
            return self.place + 1 - 2 * self.core
        one, other = 1 << step, 1 << (self.bits - step)
        flipped = [self.place + power * (1 - 2 * ((self.place // power) % 2)) for power in (one, other)]
        return jnp.where(self.core == 0, *flipped)

    def position(self, index):
        if self.bits == 0:
            return 0
        core = index % 2
        place = jnp.where(self.core == core, 1 << (self.bits - 1), 0)
        for step in range(1, self.bits):
            power = 1 << (step if core == 0 else self.bits - step)
            differs = (self.place // power + index // power) % 2
            place = place + differs * (1 << (self.bits - 1 - step))
        return place

    def barrier(self):
        if self.bits + self.n_gen == 1:
            return
        semaphore = pltpu.get_barrier_semaphore()
        for k in range(1, self.n_dp):
            pl.semaphore_signal(
                semaphore, inc=1,
                device_id={"dp": (self.place + k) % self.n_dp, "gen": self.at_line},
                device_id_type=pl.DeviceIdType.MESH,
            )
        amount = self.n_dp - 1
        if self.n_gen > 1:
            ends = ((self.at_line > 0, -1), (self.at_line < self.n_gen - 1, 1))
            for there, towards in ends:
                @pl.when(there)
                def _():
                    pl.semaphore_signal(
                        semaphore, inc=1,
                        device_id={"dp": self.place, "gen": self.at_line + towards},
                        device_id_type=pl.DeviceIdType.MESH,
                    )
                amount = amount + jnp.where(there, 1, 0)
        pl.semaphore_wait(semaphore, amount)

    def sized(self, unit, act):
        if isinstance(unit, int):
            act(16 if unit in self.small else self.rows)
            return
        is_small = unit == self.small[0]
        for one in self.small[1:]:
            is_small = is_small | (unit == one)
        pl.when(is_small)(functools.partial(act, 16))
        pl.when(~is_small)(functools.partial(act, self.rows))

    def halving(self, step, unit, rows):
        refs, many = self.refs, self.n_dp >> (step + 1)
        if step == 0:
            source = refs.unit.at[unit % self.unit_ring, pl.ds(0, many), pl.ds(0, rows)]
        else:
            source = refs.held[step - 1].at[unit % self.lags[step], pl.ds(many, many), pl.ds(0, rows)]
        slot = unit % self.ring
        return pltpu.make_async_remote_copy(
            src_ref=source,
            dst_ref=refs.into[step].at[slot, :, pl.ds(0, rows)],
            send_sem=refs.send.at[step, slot],
            recv_sem=refs.recv.at[step, slot],
            device_id={"dp": self.partners[step], "gen": self.at_line},
            device_id_type=pl.DeviceIdType.MESH,
        )

    def along(self, i, unit, towards, rows):
        slot = unit % self.line_ring
        step = self.bits + i
        return pltpu.make_async_remote_copy(
            src_ref=self.refs.total.at[unit % self.sum_ring, pl.ds(0, rows)],
            dst_ref=self.refs.line[i].at[slot, pl.ds(0, rows)],
            send_sem=self.refs.send.at[step, slot],
            recv_sem=self.refs.recv.at[step, slot],
            device_id={"dp": self.place, "gen": self.at_line + towards},
            device_id_type=pl.DeviceIdType.MESH,
        )

    def roles(self, i):
        count = self.n_gen
        half = count // 2
        if i < half - 1:
            return [(i, 1), (count - 1 - i, -1)], [i + 1, count - 2 - i], True
        if i == half - 1:
            return [(half - 1, 1), (half, -1)], [half - 1, half], True
        j = count - 2 - i
        return [(j + 1, -1), (count - 2 - j, 1)], [j, count - 1 - j], False

    def stage(self, s, unit, out_ref):
        refs, bits = self.refs, self.bits
        if s == 0:
            if bits:
                self.sized(unit, lambda rows: self.halving(0, unit, rows).start())
            return
        if s <= bits:
            self.sized(unit, lambda rows: self.halving(s - 1, unit, rows).wait())
            received = refs.into[s - 1].at[unit % self.ring]
            many = self.n_dp >> s
            if s == 1:
                kept = refs.unit.at[unit % self.unit_ring, pl.ds(many, many)]
            else:
                kept = refs.held[s - 2].at[unit % self.lags[s - 1], pl.ds(0, many)]
            if s < bits:
                refs.held[s - 1][unit % self.lags[s]] = kept[...] + received[...]
                self.sized(unit, lambda rows: self.halving(s, unit, rows).start())
                return
            refs.total[unit % self.sum_ring] = kept[0] + received[0]
        i = s - bits
        total = refs.total.at[unit % self.sum_ring]
        if i > 0:
            senders, receivers, adds = self.roles(i - 1)
            for sender, towards in senders:
                @pl.when(self.at_line == sender)
                def _():
                    self.sized(
                        unit, lambda rows: self.along(i - 1, unit, towards, rows).wait_send()
                    )

            @pl.when((self.at_line == receivers[0]) | (self.at_line == receivers[1]))
            def _():
                back = jnp.where(self.at_line == 0, 1, -1)
                self.sized(unit, lambda rows: self.along(i - 1, unit, back, rows).wait_recv())
                incoming = refs.line[i - 1].at[unit % self.line_ring]
                if adds:
                    total[...] = total[...] + incoming[...]
                else:
                    total[...] = incoming[...]
        if i < self.n_gen - 1:
            senders, _, _ = self.roles(i)
            for sender, towards in senders:
                @pl.when(self.at_line == sender)
                def _():
                    self.sized(unit, lambda rows: self.along(i, unit, towards, rows).start())
        else:
            out_ref[unit] = total[...]

    def put(self, unit, values, start=0):
        target = self.refs.unit.at[unit % self.unit_ring]
        stop = start + values.shape[1]
        for i in range(self.n_dp):
            part = values[i * self.rows : (i + 1) * self.rows].astype(LOW)
            target[self.positions[i], :, start:stop] = part

    def send(self, unit, out_ref):
        if self.bits + self.n_gen == 1:
            out_ref[unit] = self.refs.unit[unit % self.unit_ring, 0]
            return
        self.slot(unit, out_ref)
        self.stage(0, unit, out_ref)

    def drain(self, out_ref):
        def one(t, carried):
            self.slot(t, out_ref)
            return carried

        if self.bits + self.n_gen > 1:
            lax.fori_loop(self.units, self.slots, one, 0)

    def slot(self, t, out_ref):
        for s in reversed(range(1, self.final + 1)):
            unit = t - self.at[s]

            @pl.when((unit >= 0) & (unit < self.units))
            def _():
                self.stage(s, unit, out_ref)


class Shared:
    def __init__(self, plan, refs):
        self.plan, (self.own, self.all, self.sends, self.recvs) = plan, refs

    @staticmethod
    def scratch(n_dp, rows, features):
        many = max(n_dp - 1, 1)
        return (
            pltpu.VMEM((rows, features), LOW),
            pltpu.VMEM((n_dp, rows, features), LOW),
            pltpu.SemaphoreType.DMA((many,)),
            pltpu.SemaphoreType.DMA((many,)),
        )

    def copy(self, k):
        plan = self.plan
        return pltpu.make_async_remote_copy(
            src_ref=self.own,
            dst_ref=self.all.at[plan.place],
            send_sem=self.sends.at[k - 1],
            recv_sem=self.recvs.at[k - 1],
            device_id={"dp": (plan.place + k) % plan.n_dp, "gen": plan.at_line},
            device_id_type=pl.DeviceIdType.MESH,
        )

    def start(self, weights, vectors):
        plan = self.plan
        features = self.own.shape[1]
        rows, more = weights.shape[0], vectors.shape[0]
        for j in range(plan.n_gen):
            @pl.when(plan.at_line == j)
            def _():
                columns = slice(j * features, (j + 1) * features)
                self.own[:rows] = weights[:, columns]
                self.own[rows : rows + more] = vectors[:, columns]
        for k in range(1, plan.n_dp):
            self.copy(k).start()
        self.all[plan.place] = self.own[...]

    def finish(self, weights_ref, vectors_ref):
        for k in range(1, self.plan.n_dp):
            self.copy(k).wait()
        rows = self.plan.rows
        weights_ref[...] = self.all[:, :rows]
        vectors_ref[...] = self.all[:, rows:]


def gen_barrier(line, n_gen):
    semaphore = pltpu.get_barrier_semaphore()
    for k in range(1, n_gen):
        pl.semaphore_signal(
            semaphore, inc=1, device_id={"gen": (line + k) % n_gen},
            device_id_type=pl.DeviceIdType.MESH,
        )
    pl.semaphore_wait(semaphore, n_gen - 1)


def gen_copy(source, target, sends, recvs, line, k, n_gen):
    return pltpu.make_async_remote_copy(
        src_ref=source,
        dst_ref=target.at[line],
        send_sem=sends.at[k - 1],
        recv_sem=recvs.at[k - 1],
        device_id={"gen": (line + k) % n_gen},
        device_id_type=pl.DeviceIdType.MESH,
    )


def sum_gen_kernel(n_gen, part_ref, out_ref, parts, sends, recvs):
    line = lax.axis_index("gen")
    gen_barrier(line, n_gen)
    for k in range(1, n_gen):
        gen_copy(part_ref, parts, sends, recvs, line, k, n_gen).start()
    parts[line] = part_ref[...]
    for k in range(1, n_gen):
        gen_copy(part_ref, parts, sends, recvs, line, k, n_gen).wait()
    total = parts[0]
    for j in range(1, n_gen):
        total = total + parts[j]
    out_ref[...] = total


def sum_gen(part):
    n_gen = lax.axis_size("gen")
    if n_gen == 1:
        return part
    return pl.pallas_call(
        functools.partial(sum_gen_kernel, n_gen),
        in_specs=[pl.BlockSpec(memory_space=pltpu.VMEM)],
        out_specs=pl.BlockSpec(memory_space=pltpu.VMEM),
        out_shape=jax.ShapeDtypeStruct(part.shape, part.dtype),
        scratch_shapes=[
            pltpu.VMEM((n_gen,) + part.shape, part.dtype),
            pltpu.SemaphoreType.DMA((n_gen - 1,)),
            pltpu.SemaphoreType.DMA((n_gen - 1,)),
        ],
        compiler_params=pltpu.CompilerParams(collective_id=2, has_side_effects=True),
        name="sum_gen",
    )(part)


class Operands(NamedTuple):
    cotangent: object
    cross_hidden: object
    dec_hidden: object
    encoded: object
    enc_hidden: object
    dec_rows: object
    enc_rows: object
    enc_qkv: object
    enc_proj: object
    enc_up: object
    enc_down: object
    dec_qkv: object
    dec_self_proj: object
    dec_cross_q: object
    dec_cross_kv: object
    dec_cross_proj: object
    dec_up: object
    dec_down: object
    enc_attn: Attended
    dec_attn: Attended
    cross_attn: Attended
    enc_ffn: Fed
    dec_ffn: Fed
    small: object


class Small(NamedTuple):
    enc_norms: object
    dec_norms: object
    adapters: object
    vectors: object
    wanted: object


class Results(NamedTuple):
    sums: object
    pair_weights: object
    pair_vectors: object
    grad_dec_rows: object
    grad_enc_rows: object


class Held(NamedTuple):
    total: object
    total_memory: object
    grad_low: object
    grad_a: object
    grad_b: object
    adapters: object
    vectors: object
    gains: object
    transfer: TransferRefs
    shared: object


class Backward:
    def __init__(self, plan, up_scale, bottleneck, tasks, refs, small, scratch, out_ref):
        self.plan, self.up_scale, self.bottleneck, self.tasks = plan, up_scale, bottleneck, tasks
        self.refs, self.small, self.scratch, self.out_ref = refs, small, scratch, out_ref

    def send(self, unit):
        self.plan.send(unit, self.out_ref)

    def attention(
        self, first_unit, grad_ref, gain_rows, x, memory, stored, weights, finish, after_first=None
    ):
        cross = memory is not None
        plan, scratch = self.plan, self.scratch
        total_x, total_memory, grad_low = scratch.total, scratch.total_memory, scratch.grad_low
        length, width = x.shape
        groups = width // GROUP
        columns = pl.BlockSpec((length, GROUP), lambda g: (0, g))
        rows = pl.BlockSpec((GROUP, length), lambda g: (g, 0))

        def weight_spec(offset):
            return pl.BlockSpec((width, GROUP), lambda g: (0, offset + g))

        def body(
            x_ref, x_t_ref, q_t_ref, k_ref, v_ref, mixed_t_ref, probs_ref,
            wq_ref, wk_ref, wv_ref, wo_ref, *more,
        ):
            memory_ref, memory_t_ref = more if cross else (x_ref, x_t_ref)
            step = pl.program_id(0)

            @pl.when(step == 0)
            def _():
                grad_low[...] = grad_ref[...].astype(LOW)
                total_x[...] = jnp.zeros_like(total_x)
                if cross:
                    total_memory[...] = jnp.zeros_like(total_memory)
                plan.put(first_unit, dot_nn(mixed_t_ref[...], grad_low[...]))
                self.send(first_unit)
                if after_first is not None:
                    after_first()

            grad_mixed = dot_nt(grad_low[...], wo_ref[...]).astype(LOW)
            grad_mixed_t = grad_mixed.T
            lanes = first_half((length, 2 * HD))
            heads = range(4)

            def pair_of(ref, head):
                pair = head // 2
                return ref[:, pair * 2 * HD : (pair + 1) * 2 * HD]

            def rows_of(ref, head):
                return ref[head * HD : (head + 1) * HD, :]

            grad_probs = []
            for head in heads:
                mine = jnp.where(
                    lanes if head % 2 == 0 else ~lanes, pair_of(grad_mixed, head), LOW(0)
                )
                grad_probs.append(dot_nt(mine, pair_of(v_ref, head)))
            probs = probs_ref[...].astype(WIDE)
            product = probs * jnp.stack(grad_probs)
            grad_scores = (
                product - probs * jnp.sum(product, axis=-1, keepdims=True)
            ).astype(LOW)
            halves = [dot_nn(grad_scores[head], pair_of(k_ref, head)) for head in heads]
            grad_q = [
                jnp.where(lanes, halves[head], halves[head + 1]) * HD ** (-0.5)
                for head in heads[::2]
            ]
            grad_k = [
                dot_nn(rows_of(q_t_ref, head), grad_scores[head]) * HD ** (-0.5) for head in heads
            ]
            grad_v = [dot_nn(rows_of(grad_mixed_t, head), probs_ref[head]) for head in heads]
            low_q = jnp.concatenate(grad_q, axis=1).astype(LOW)
            low_k = jnp.concatenate(grad_k, axis=0).astype(LOW).T
            low_v = jnp.concatenate(grad_v, axis=0).astype(LOW).T
            unit = first_unit + 1 + step
            plan.put(unit, dot_nn(x_t_ref[...], low_q), 0)
            plan.put(unit, dot_nn(memory_t_ref[...], low_k), GROUP)
            plan.put(unit, dot_nn(memory_t_ref[...], low_v), 2 * GROUP)
            self.send(unit)
            total_x[...] += dot_nt(low_q, wq_ref[...])
            total_source = total_memory if cross else total_x
            total_source[...] += dot_nt(low_k, wk_ref[...]) + dot_nt(low_v, wv_ref[...])

            @pl.when(step == groups - 1)
            def _():
                x_gain, memory_gain = gain_rows
                grad_values, grad_gain = rms_backward(
                    x_ref[...].astype(WIDE), self.gain(x_gain), total_x[...]
                )
                scratch.gains[x_gain : x_gain + 1] = grad_gain
                finish(grad_ref[...] + grad_values)
                if cross:
                    grad_values, grad_gain = rms_backward(
                        memory_ref[...], self.gain(memory_gain), total_memory[...]
                    )
                    scratch.gains[memory_gain : memory_gain + 1] = grad_gain
                    scratch.grad_b[...] = grad_values

        whole_tokens, whole_turned = whole((length, width)), whole((width, length))
        pltpu.emit_pipeline(
            body,
            grid=(groups,),
            in_specs=[
                whole_tokens, whole_turned, rows, columns, columns, whole_turned,
                pl.BlockSpec((4, length, length), lambda g: (g, 0, 0)),
                weight_spec(weights[0][1] * groups),
                weight_spec(weights[1][1] * groups),
                weight_spec(weights[2][1] * groups),
                pl.BlockSpec((GROUP, width), lambda g: (g, 0)),
            ]
            + ([whole_tokens, whole_turned] if cross else []),
        )(
            x, stored.x_t, stored.q_t, stored.keys, stored.values, stored.mixed_t, stored.probs,
            weights[0][0], weights[1][0], weights[2][0], weights[3],
            *([memory, stored.memory_t] if cross else []),
        )

    def gain(self, row):
        small = self.small
        return row_of(small.enc_norms, row) if row < 2 else row_of(small.dec_norms, row - 2)

    def feed_forward(
        self, first_unit, grad, x, gain_row, layer, w_up, w_down, stored, finish, after_adapter=None
    ):
        plan, small, scratch, up_scale = self.plan, self.small, self.scratch, self.up_scale
        total, grad_low = scratch.total, scratch.grad_low
        length, width = x.shape
        n_dp, blocks, rows, _ = stored.active_t.shape

        def body(x_ref, ffn_ref, x_t_ref, up_ref, down_ref, active_t_ref, slope_ref, *more):
            grad_ref = more[0] if more else scratch.grad_b
            step = pl.program_id(0)

            @pl.when(step == 0)
            def _():
                grad = grad_ref[...].astype(WIDE)
                vectors = small.vectors[layer].astype(WIDE)
                lower, upper = small.adapters[layer, 0], small.adapters[layer, 1]
                normed, scale = layer_parts(ffn_ref[...])
                gain = 1.0 + vectors[1:2]
                low = (normed * gain + vectors[2:3]).astype(LOW)
                inner = dot_nt(low, lower)
                cumulative, density = gelu_parts(inner)
                gate = (inner * cumulative).astype(LOW)
                scaled = (grad * up_scale).astype(LOW)
                scratch.adapters[layer, 1] = dot_nn(gate.T, scaled)
                grad_gate = dot_nt(scaled, upper)
                grad_inner = (grad_gate * (cumulative + inner * density)).astype(LOW)
                scratch.adapters[layer, 0] = dot_nn(grad_inner.T, low)
                grad_normed = dot_nn(grad_inner, lower)
                keep = scratch.vectors
                keep[3 * layer : 3 * layer + 1] = jnp.sum(grad, axis=0, keepdims=True)
                keep[3 * layer + 1 : 3 * layer + 2] = jnp.sum(
                    grad_normed * normed, axis=0, keepdims=True
                )
                keep[3 * layer + 2 : 3 * layer + 3] = jnp.sum(grad_normed, axis=0, keepdims=True)
                pulled = grad_normed * gain
                pulled = scale * (
                    pulled
                    - jnp.mean(pulled, axis=-1, keepdims=True)
                    - normed * jnp.mean(pulled * normed, axis=-1, keepdims=True)
                )
                grad_low[...] = (grad + pulled).astype(LOW)
                total[...] = jnp.zeros_like(total)
                if after_adapter is not None:
                    after_adapter()

            unit = first_unit + 2 * step
            plan.put(unit, dot_nn(join_rows(active_t_ref), grad_low[...]))
            self.send(unit)
            grad_active = dot_nt(grad_low[...], down_ref[...])
            grad_before = (grad_active * slope_ref[...].astype(WIDE)).astype(LOW)
            plan.put(unit + 1, dot_nn(x_t_ref[...], grad_before))
            self.send(unit + 1)
            total[...] += dot_nt(grad_before, up_ref[...])

            @pl.when(step == blocks - 1)
            def _():
                grad_values, grad_gain = rms_backward(
                    x_ref[...], self.gain(gain_row), total[...]
                )
                scratch.gains[gain_row : gain_row + 1] = grad_gain
                finish(grad_ref[...].astype(WIDE) + grad_values)

        tokens = whole((length, width))
        pltpu.emit_pipeline(
            body,
            grid=(blocks,),
            in_specs=[
                tokens, tokens, whole((width, length)),
                pl.BlockSpec((width, width), lambda j: (0, j)),
                pl.BlockSpec((width, width), lambda j: (j, 0)),
                pl.BlockSpec((n_dp, 1, rows, length), lambda j: (0, j, 0, 0)),
                pl.BlockSpec((length, width), lambda j: (0, j)),
            ]
            + ([] if grad is None else [tokens]),
        )(
            x, stored.ffn, stored.x_t, w_up, w_down, stored.active_t, stored.slope,
            *([] if grad is None else [grad]),
        )

    def own_rows(self, values, rows_per_task, first, count):
        parts = []
        while count:
            task, offset = divmod(first, rows_per_task)
            some = min(count, rows_per_task - offset)
            if task < self.tasks:
                weight = self.small.wanted[0:1, 2 * task : 2 * task + 1]
                parts.append(values[offset : offset + some] * weight)
            else:
                parts.append(jnp.zeros((some, values.shape[1]), WIDE))
            first, count = first + some, count - some
        return parts[0] if len(parts) == 1 else jnp.concatenate(parts, axis=0)

    def send_adapters(self, unit):
        plan, kept, size = self.plan, self.scratch.adapters, self.bottleneck
        values = jnp.concatenate(
            [kept[layer, part, :size] for layer in range(kept.shape[0]) for part in range(2)], axis=0
        )
        target = plan.refs.unit.at[unit % plan.unit_ring]
        for i in range(plan.n_dp):
            part = self.own_rows(values, values.shape[0], i * plan.rows, plan.rows)
            target[plan.positions[i]] = part.astype(LOW)
        self.send(unit)

    def send_vectors(self, unit, vector_rows):
        plan = self.plan
        values = self.scratch.vectors[:6]
        spare = -vector_rows % 16
        for i in range(plan.n_dp):
            part = self.own_rows(values, 6, i * vector_rows, vector_rows)
            if spare:
                part = jnp.concatenate([part, jnp.zeros((spare, plan.width), WIDE)], axis=0)
            target = plan.refs.unit.at[unit % plan.unit_ring, plan.positions[i]]
            target[: part.shape[0]] = part.astype(LOW)
        self.send(unit)

    def send_gains(self, unit):
        plan = self.plan
        rows, width = plan.rows, plan.width
        for i in range(plan.n_dp):
            part = self.scratch.gains[:6, i * rows : (i + 1) * rows]
            if rows < width:
                part = jnp.concatenate([part, jnp.zeros((6, width - rows), WIDE)], axis=1)
            part = jnp.concatenate([part, jnp.zeros((10, width), WIDE)], axis=0)
            target = plan.refs.unit.at[unit % plan.unit_ring, plan.positions[i]]
            target[0:16] = part.astype(LOW)
        self.send(unit)


def backward_kernel(plan, up_scale, bottleneck, tasks, vector_rows, trees, *leaves):
    counts = [tree.num_leaves for tree in trees]
    parts, start = [], 0
    for tree, count in zip(trees, counts):
        parts.append(jax.tree.unflatten(tree, leaves[start : start + count]))
        start += count
    refs, out, scratch = parts
    plan.bind(scratch.transfer)
    plan.barrier()
    work = Backward(plan, up_scale, bottleneck, tasks, refs, refs.small, scratch, out.sums)
    shared = Shared(plan, scratch.shared)
    grad_a, grad_b = scratch.grad_a, scratch.grad_b

    def into(ref):
        def finish(values):
            ref[...] = values.astype(ref.dtype)

        return finish

    def adapters():
        work.send_adapters(12)
        work.send_vectors(13, vector_rows)

    def share():
        shared.start(out.sums.at[12], out.sums.at[13, pl.ds(0, 16)])

    early = 13 + plan.at[plan.final] <= 26
    work.feed_forward(
        0, refs.cotangent, refs.cross_hidden, 4, 1, refs.dec_up, refs.dec_down, refs.dec_ffn,
        into(grad_a),
    )
    work.attention(
        8, grad_a, (3, 5), refs.dec_hidden, refs.encoded, refs.cross_attn,
        ((refs.dec_cross_q, 0), (refs.dec_cross_kv, 0), (refs.dec_cross_kv, 1), refs.dec_cross_proj),
        into(grad_a),
    )
    work.feed_forward(
        14, None, refs.enc_hidden, 1, 0, refs.enc_up, refs.enc_down, refs.enc_ffn, into(grad_b),
        after_adapter=adapters,
    )
    work.attention(
        22, grad_a, (2, None), refs.dec_rows, None, refs.dec_attn,
        ((refs.dec_qkv, 0), (refs.dec_qkv, 1), (refs.dec_qkv, 2), refs.dec_self_proj),
        into(out.grad_dec_rows),
    )
    work.attention(
        26, grad_b, (0, None), refs.enc_rows, None, refs.enc_attn,
        ((refs.enc_qkv, 0), (refs.enc_qkv, 1), (refs.enc_qkv, 2), refs.enc_proj),
        into(out.grad_enc_rows), after_first=share if early else None,
    )
    work.send_gains(30)
    plan.drain(out.sums)
    if not early:
        share()
    shared.finish(out.pair_weights, out.pair_vectors)


def backward(operands, features, up_scale, bottleneck, tasks, vector_rows):
    n_dp, n_gen = lax.axis_size("dp"), lax.axis_size("gen")
    length, width = operands.enc_rows.shape
    rows = width // n_dp
    plan = Transfer(31, (13, 30), n_dp, n_gen, rows, width, LAGS)

    def blocked(fed):
        return fed._replace(active_t=fed.active_t.reshape(n_dp, -1, rows, length))

    operands = operands._replace(
        enc_ffn=blocked(operands.enc_ffn), dec_ffn=blocked(operands.dec_ffn)
    )
    tokens = pltpu.VMEM((length, width), WIDE)
    shared_rows = rows + 16
    held = Held(
        total=tokens,
        total_memory=tokens,
        grad_low=pltpu.VMEM((length, width), LOW),
        grad_a=tokens,
        grad_b=tokens,
        adapters=pltpu.VMEM(operands.small.adapters.shape, WIDE),
        vectors=pltpu.VMEM((8, width), WIDE),
        gains=pltpu.VMEM((8, width), WIDE),
        transfer=plan.scratch(),
        shared=Shared.scratch(n_dp, shared_rows, features),
    )
    shape = jax.ShapeDtypeStruct
    results = Results(
        sums=shape((plan.units, rows, width), LOW),
        pair_weights=shape((n_dp, rows, features), LOW),
        pair_vectors=shape((n_dp, 16, features), LOW),
        grad_dec_rows=shape((length, width), LOW),
        grad_enc_rows=shape((length, width), LOW),
    )
    in_vmem = pl.BlockSpec(memory_space=pltpu.VMEM)
    in_hbm = pl.BlockSpec(memory_space=pl.ANY)
    specs = jax.tree.map(lambda _: in_hbm, operands)
    specs = specs._replace(small=jax.tree.map(lambda _: in_vmem, operands.small))
    flat, in_tree = jax.tree.flatten(operands)
    scratch, scratch_tree = jax.tree.flatten(held)
    out, out_tree = jax.tree.flatten(results)
    remote = n_dp * n_gen > 1
    outs = pl.pallas_call(
        functools.partial(
            backward_kernel, plan, up_scale, bottleneck, tasks, vector_rows,
            (in_tree, out_tree, scratch_tree),
        ),
        in_specs=jax.tree.leaves(specs),
        out_specs=[in_vmem] * len(out),
        out_shape=out,
        scratch_shapes=scratch,
        compiler_params=pltpu.CompilerParams(
            vmem_limit_bytes=VMEM_LIMIT,
            **(dict(collective_id=0, has_side_effects=True) if remote else {}),
        ),
        cost_estimate=pl.CostEstimate(
            flops=100 * length * width * width, bytes_accessed=160 * width * width,
            transcendentals=0,
        ),
        name="backward",
    )(*flat)
    return jax.tree.unflatten(out_tree, outs)


class Gradients(NamedTuple):
    enc_norms: object
    enc_qkv: object
    enc_proj: object
    enc_up: object
    enc_down: object
    dec_norms: object
    dec_qkv: object
    dec_self_proj: object
    dec_cross_q: object
    dec_cross_kv: object
    dec_cross_proj: object
    dec_up: object
    dec_down: object


def unpack_kernel(sums_ref, dec_ref, enc_ref, *outs):
    out = Gradients(*outs[:13])
    outs[13][...] = dec_ref[...]
    outs[14][...] = enc_ref[...]
    size = out.enc_norms.shape[1]
    gains = sums_ref[30, 0:16, :].astype(WIDE)

    @pl.when(pl.program_id(0) == 0)
    def _():
        out.enc_norms[...] = gains[0:2, :size]
        out.dec_norms[...] = gains[2:6, :size]

    def plain(target, unit):
        target[...] = sums_ref[unit].astype(WIDE)

    def joint(target, first, parts):
        for at, part in enumerate(parts):
            for g in range(3):
                start = (3 * at + g) * GROUP
                target[:, start : start + GROUP] = sums_ref[
                    first + g, :, part * GROUP : (part + 1) * GROUP
                ].astype(WIDE)

    def beside(target, first):
        width = sums_ref.shape[2]
        for j in range(target.shape[1] // width):
            target[:, j * width : (j + 1) * width] = sums_ref[first + 2 * j].astype(WIDE)

    def below(target, first):
        for j in range(target.shape[0]):
            target[j] = sums_ref[first + 2 * j].astype(WIDE)

    below(out.dec_down, 0)
    beside(out.dec_up, 1)
    plain(out.dec_cross_proj, 8)
    joint(out.dec_cross_q, 9, (0,))
    joint(out.dec_cross_kv, 9, (1, 2))
    below(out.enc_down, 14)
    beside(out.enc_up, 15)
    plain(out.dec_self_proj, 22)
    joint(out.dec_qkv, 23, (0, 1, 2))
    plain(out.enc_proj, 26)
    joint(out.enc_qkv, 27, (0, 1, 2))


def unpack(sums, grad_dec_rows, grad_enc_rows, inner):
    units, rows, width = sums.shape
    length = grad_dec_rows.shape[0]
    steps = rows // 32 if rows % 32 == 0 else 1
    block = rows // steps
    while length % (16 * steps):
        steps, block = 1, rows
    shape = jax.ShapeDtypeStruct

    def matrix(columns):
        return shape((rows, columns), WIDE), pl.BlockSpec((block, columns), lambda i: (i, 0))

    downs = inner // width
    down = (
        shape((downs, rows, width), WIDE),
        pl.BlockSpec((downs, block, width), lambda i: (0, i, 0)),
    )
    tokens = pl.BlockSpec((length // steps, width), lambda i: (i, 0))

    def norms(count):
        return shape((count, rows), WIDE), whole((count, rows))

    made = Gradients(
        enc_norms=norms(2), enc_qkv=matrix(3 * width), enc_proj=matrix(width),
        enc_up=matrix(inner), enc_down=down, dec_norms=norms(4), dec_qkv=matrix(3 * width),
        dec_self_proj=matrix(width), dec_cross_q=matrix(width), dec_cross_kv=matrix(2 * width),
        dec_cross_proj=matrix(width), dec_up=matrix(inner), dec_down=down,
    )
    outs = pl.pallas_call(
        unpack_kernel,
        grid=(steps,),
        in_specs=[pl.BlockSpec((units, block, width), lambda i: (0, i, 0)), tokens, tokens],
        out_specs=[spec for _, spec in made] + [tokens, tokens],
        out_shape=[one for one, _ in made] + [shape((length, width), LOW)] * 2,
        compiler_params=pltpu.CompilerParams(vmem_limit_bytes=VMEM_LIMIT),
        cost_estimate=pl.CostEstimate(
            flops=0, bytes_accessed=6 * units * rows * width, transcendentals=0
        ),
        name="unpack",
    )(sums, grad_dec_rows, grad_enc_rows)
    grads = Gradients(*outs[:13])
    grads = grads._replace(
        enc_down=grads.enc_down.reshape(-1, width), dec_down=grads.dec_down.reshape(-1, width)
    )
    return grads, outs[13], outs[14]


def gelu_exact(values):
    return jax.nn.gelu(values, approximate=False)


def body(
    enc_input,
    dec_input,
    enc_segments,
    dec_segments,
    task_ids,
    cotangent,
    enc_norms,
    enc_qkv,
    enc_proj,
    enc_up,
    enc_down,
    dec_norms,
    dec_qkv,
    dec_self_proj,
    dec_cross_q,
    dec_cross_kv,
    dec_cross_proj,
    dec_up,
    dec_down,
    task_emb,
    layer_emb,
    proj_task,
    gen_weight,
    gen_vector,
):
    _, length, width = enc_input.shape
    layer_count = layer_emb.shape[0]
    pair_count = task_emb.shape[0] * layer_count
    bottleneck = gen_weight.shape[1] // 2
    up_scale = (width / bottleneck) ** 0.5

    def source_of(task_table, layer_table, projection):
        mixed_in = (
            jnp.dot(task_table, projection, precision=HIGHEST)[:, None, :] + layer_table[None, :, :]
        )
        return gelu_exact(mixed_in).reshape(pair_count, -1)

    source, source_pull = jax.vjp(source_of, task_emb, layer_emb, proj_task)
    source_low = source.astype(LOW)
    pieces, more_pieces = [
        jnp.einsum("th,hkd->tkd", source_low, part, preferred_element_type=WIDE).astype(LOW)
        for part in (gen_weight, gen_vector)
    ]
    first_pair = task_ids[0] * layer_count
    wanted = jnp.arange(8)[:, None] + first_pair == jnp.arange(128)[None, :]
    wanted = wanted.astype(WIDE)

    enc_rows, dec_rows = enc_input[0], dec_input[0]
    enc_joint = [(enc_qkv, 0), (enc_qkv, 1), (enc_qkv, 2)]
    dec_joint = [(dec_qkv, 0), (dec_qkv, 1), (dec_qkv, 2)]
    cross_joint = [(dec_cross_q, 0), (dec_cross_kv, 0), (dec_cross_kv, 1)]
    enc_hidden, enc_stored, adapters, vectors = attention_forward(
        enc_rows, enc_norms, (0, 0), None, enc_segments, enc_segments, enc_joint, enc_proj, False,
        gather=(wanted, pieces, more_pieces, bottleneck),
    )
    dec_hidden, dec_stored = attention_forward(
        dec_rows, dec_norms, (0, 0), None, dec_segments, dec_segments, dec_joint, dec_self_proj, True
    )
    encoded, enc_ffn_stored = feed_forward(
        enc_hidden, enc_norms, 1, enc_up, enc_down, adapters, vectors, 0, up_scale, WIDE
    )
    cross_hidden, cross_stored = attention_forward(
        dec_hidden, dec_norms, (1, 3), encoded, dec_segments, enc_segments, cross_joint,
        dec_cross_proj, False,
    )
    decoded, dec_ffn_stored = feed_forward(
        cross_hidden, dec_norms, 2, dec_up, dec_down, adapters, vectors, 1, up_scale, LOW
    )

    n_dp = lax.axis_size("dp")
    rows = width // n_dp
    features = gen_weight.shape[2]
    vector_rows = -(-pair_count * 3 // n_dp)
    small = Small(enc_norms, dec_norms, adapters, vectors, wanted)
    operands = Operands(
        cotangent[0], cross_hidden, dec_hidden, encoded, enc_hidden, dec_rows, enc_rows,
        enc_qkv, enc_proj, enc_up, enc_down, dec_qkv, dec_self_proj, dec_cross_q, dec_cross_kv,
        dec_cross_proj, dec_up, dec_down,
        enc_stored, dec_stored, cross_stored, enc_ffn_stored, dec_ffn_stored, small,
    )
    result = backward(
        operands, features, up_scale, bottleneck, task_emb.shape[0], vector_rows
    )
    pair_weights = result.pair_weights.reshape(pair_count, 2 * bottleneck, features)
    pair_vectors = result.pair_vectors[:, :vector_rows].reshape(-1, features)
    pair_vectors = pair_vectors[: pair_count * 3].reshape(pair_count, 3, features)
    grad_gen_weight, grad_gen_vector = [
        jnp.einsum("th,tkd->hkd", source_low, part, preferred_element_type=WIDE)
        for part in (pair_weights, pair_vectors)
    ]
    part_source = sum(
        jnp.einsum("tkd,hkd->th", part, made, preferred_element_type=WIDE)
        for part, made in ((pair_weights, gen_weight), (pair_vectors, gen_vector))
    )
    grad_source = sum_gen(part_source)
    grad_task_emb, grad_layer_emb, grad_proj_task = source_pull(grad_source)

    grads, grad_dec_rows, grad_enc_rows = unpack(
        result.sums, result.grad_dec_rows, result.grad_enc_rows, enc_up.shape[1]
    )
    return (
        decoded[None],
        grad_enc_rows[None],
        grad_dec_rows[None],
        *grads,
        grad_task_emb,
        grad_layer_emb,
        grad_proj_task,
        grad_gen_weight,
        grad_gen_vector,
    )


def solution(mesh):
    in_specs = (
        P(("dp", "gen"), None, None),
        P(("dp", "gen"), None, None),
        P(("dp", "gen"), None),
        P(("dp", "gen"), None),
        P(("dp", "gen")),
        P(("dp", "gen"), None, None),
        P(),
        P(),
        P(),
        P(),
        P(),
        P(),
        P(),
        P(),
        P(),
        P(),
        P(),
        P(),
        P(),
        P(),
        P(),
        P(),
        P(None, None, "gen"),
        P(None, None, "gen"),
    )
    out_specs = (
        P(("dp", "gen"), None, None),
        P(("dp", "gen"), None, None),
        P(("dp", "gen"), None, None),
        P(None, "dp"),
        P("dp", None),
        P("dp", None),
        P("dp", None),
        P("dp", None),
        P(None, "dp"),
        P("dp", None),
        P("dp", None),
        P("dp", None),
        P("dp", None),
        P("dp", None),
        P("dp", None),
        P("dp", None),
        P(),
        P(),
        P(),
        P(None, None, "gen"),
        P(None, None, "gen"),
    )
    return jax.shard_map(body, mesh=mesh, in_specs=in_specs, out_specs=out_specs, check_vma=False)
```

time: 1200 us -> 330 us (0.28)
  waiting for transfers between devices: 600 us -> 0 us
  Pallas kernels: 0 us -> 306 us
  matrix products: 291 us -> 11.6 us
  local copies, waits for them, and re-layouts: 111 us -> 1.65 us
  other arithmetic: 93.1 us -> 2.7 us
  blocking collectives: 84 us -> 0 us
  between operations: 17.5 us -> 1.85 us
    reduce_scatter x11 -> x0, waiting for transfers between devices: 374 us -> none  [the longest x1 58.2 us: body(): lax.psum_scatter(grad_enc_up.astype(jnp.bfloat16), 'dp', scatter_dimensio...]
    pallas_call x0 -> x8, Pallas kernels: none -> 306 us  [the longest x1 206 us: backward(): pl.pallas_call(functools.partial(backward_kernel, plan, up_scale, bottlen...]
    dot_general x73 -> x6, matrix products: 287 us -> 9.05 us  [the longest x2 4.18 us: body(): jnp.einsum('th,tkd->hkd', source_low, part, preferred_element_type=WIDE)]
    psum x2 -> x0, waiting for transfers between devices: 162 us -> none  [the longest x1 154 us: body(): lax.psum(grad_enc_qkv.astype(jnp.bfloat16), 'gen').astype(jnp.float32)]
    unnamed x22 -> x0, waiting for transfers between devices: 64.3 us -> none
    unnamed x372 -> x14, local copies, waits for them, and re-layouts: 61.3 us -> 0.05 us
    convert_element_type x26 -> x2, other arithmetic: 53.4 us -> 1.39 us  [the longest x1 0.72 us: body(): source_low = source.astype(LOW)]
    psum x2 -> x0, blocking collectives: 49.7 us -> none  [the longest x1 37.4 us: body(): grad_source = lax.psum(part_source, ('dp', 'gen'))]
  transfers between devices with their start and end apart: 18 -> 0, of which waited for: 11 -> 0; matrix products, arithmetic and copies ran while one was open for 28% -> 0% of each run, Pallas kernels for 0% -> 0%
where the time goes in v1:
time: 330 us; the launch traced here: 324 us
  Pallas kernels  306 us (93%)
  matrix products  11.6 us (4%)
    pallas_call x1, Pallas kernels, backward(): pl.pallas_call(functools.partial(backward_kernel, plan, up_scale, bottlen...  206 us
    pallas_call x3, Pallas kernels, attention_forward(): pl.pallas_call(functools.partial(attention_forward_kernel, cross, causal,...  50.9 us
    pallas_call x2, Pallas kernels, feed_forward(): pl.pallas_call(functools.partial(feed_forward_kernel, up_scale, layer, ga...  35.4 us
    pallas_call x1, Pallas kernels, unpack(): pl.pallas_call(unpack_kernel, grid=(steps,), in_specs=[pl.BlockSpec((unit...  6.88 us
    pallas_call x1, Pallas kernels, sum_gen(): pl.pallas_call(functools.partial(sum_gen_kernel, n_gen), in_specs=[pl.Blo...  6.8 us

profile of v1, /device:TPU:0, one launch (start us, length us, event | category | flops | bytes accessed | tf_op | source)
XLA Modules:
  0.0 323.7 jit_solution(17270440572769320743)
XLA Ops:
  0.7 0.0 copy-start
  1.5 0.7 fusion.52.refs_0_.leaves_49_
  2.1 0.9 fusion.56
  3.0 0.7 multiply_convert_fusion
  3.8 1.1 convolution_convert_fusion
  4.9 0.7 copy.68.refs_2_
  5.6 0.0 copy-done
  5.6 1.3 fusion.50
  6.9 0.9 copy.86.refs_1_
  7.8 21.3 %attention_forward.4 = (f32[512,768]{1,0:T(8,128)}, bf16[768,512]{1,0:T(8,128)(2,1)}, bf16[16,128]{1,0:T(8,128)(2,1)}, bf16[768,512]{1,0:T(8,128)(2,1)}, bf16[51...) custom-call(bf16[512,768]{1,0:T(8,128)(2,1)} %bitcast.46, ...), custom_call_target="tpu_custom_call" | custom-call | flops 3221225472 | bytes 17301504 | tf_op jit(solution)/shard_map/attention_forward/pallas_call | solution.py:271
  29.1 18.1 %feed_forward.2 = (f32[512,768]{1,0:T(8,128)}, f32[512,768]{1,0:T(8,128)}, bf16[768,512]{1,0:T(8,128)(2,1)}, bf16[3072,512]{1,0:T(8,128)(2,1)}, bf16[512,3072]{1,0:T(8,128)(2,1)}) custom-call(f32[512,768]{1,0:T(8,128)} %get-tuple-element.76.x_ref.leaves_4_, bf16[2,768]{1,0:T(2,128)(2,1)} %leaves_45_.1, bf16[768,3072]{1,0:T(8,128)(2,1)} %leaves_9_.1, ...), custom_call_target="tpu_custom_call" | custom-call | flops 4831838208 | bytes 20447232 | tf_op jit(solution)/shard_map/feed_forward/pallas_call | solution.py:381
  47.1 14.2 %attention_forward.3 = (f32[512,768]{1,0:T(8,128)}, bf16[768,512]{1,0:T(8,128)(2,1)}, bf16[16,128]{1,0:T(8,128)(2,1)}, bf16[768,512]{1,0:T(8,128)(2,1)}, bf16[51...) custom-call(bf16[512,768]{1,0:T(8,128)(2,1)} %bitcast.43, ...), custom_call_target="tpu_custom_call" | custom-call | flops 3221225472 | bytes 17301504 | tf_op jit(solution)/shard_map/attention_forward/pallas_call | solution.py:271
  61.3 15.5 %attention_forward.5 = (f32[512,768]{1,0:T(8,128)}, bf16[768,512]{1,0:T(8,128)(2,1)}, bf16[768,512]{1,0:T(8,128)(2,1)}, bf16[768,512]{1,0:T(8,128)(2,1)}, bf16[5...) custom-call(f32[512,768]{1,0:T(8,128)} %get-tuple-element.75.x_ref.leav, ...), custom_call_target="tpu_custom_call" | custom-call | flops 3221225472 | bytes 17301504 | tf_op jit(solution)/shard_map/attention_forward/pallas_call | solution.py:271
  76.8 17.3 %feed_forward.3 = (bf16[512,768]{1,0:T(8,128)(2,1)}, f32[512,768]{1,0:T(8,128)}, bf16[768,512]{1,0:T(8,128)(2,1)}, bf16[3072,512]{1,0:T(8,128)(2,1)}, bf16[512,3072]{1,0:T(8,128)(2,1)}) custom-call(f32[512,768]{1,0:T(8,128)} %get-tuple-element.80.x_ref.leaves_1_, bf16[4,768]{1,0:T(4,128)(2,1)} %leaves_46_.1, bf16[768,3072]{1,0:T(8,128)(2,1)} %leaves_16_.1, ...), custom_call_target="tpu_custom_call" | custom-call | flops 4831838208 | bytes 20447232 | tf_op jit(solution)/shard_map/feed_forward/pallas_call | solution.py:381
  94.1 205.9 %backward.1 = (bf16[31,96,768]{2,1,0:T(8,128)(2,1)}, bf16[8,96,192]{2,1,0:T(8,128)(2,1)}, bf16[8,16,192]{2,1,0:T(8,128)(2,1)}, bf16[512,768]{1,0:T(8,128)(2,1)}, bf16[512,768]{1,0:T(8,128)(2,1)}) custom-call(bf16[512,768]{1,0:T(8,128)(2,1)} %bitcast.60, f32[512,768]{1,0:T(8,128)} %get-tuple-element.80.x_ref.leaves_1_, ...), custom_call_target="tpu_custom_call" | custom-call | flops 30198988800 | bytes 94371840 | tf_op jit(solution)/shard_map/backward/pallas_call | solution.py:1153
  300.0 0.0 copy-start.4
  300.0 0.0 copy-start.2
  300.1 0.0 copy-start.6
  300.1 0.0 copy-start.3
  300.1 0.0 copy-start.5
  300.1 1.7 convolution_bitcast_fusion.2
  301.8 0.0 copy-done.4
  301.8 0.0 copy-done.2
  301.8 0.8 fusion.part_ref
  302.6 6.8 %sum_gen.1 = f32[16,128]{1,0:T(8,128)} custom-call(f32[16,128]{1,0:T(8,128)} %fusion.part_ref), custom_call_target="tpu_custom_call" | custom-call | tf_op jit(solution)/shard_map/sum_gen/pallas_call | solution.py:732
  309.4 0.0 copy-done.6
  309.4 1.3 fusion.55
  310.7 0.0 copy-done.3
  310.8 0.8 fusion.57
  311.5 0.0 copy-done.5
  311.5 0.8 convolution_bitcast_fusion
  312.4 1.0 fusion.4
  313.3 0.0 copy-start.1
  313.3 6.9 %unpack.1 = (f32[2,96]{1,0:T(2,128)}, f32[96,2304]{1,0:T(8,128)}, f32[96,768]{1,0:T(8,128)}, f32[96,3072]{1,0:T(8,128)}, f32[4,96,768]{2,1,0:T(8,128)}, /*index=...) custom-call(bf16[31,96,768]{2,1,0:T(8,128)(2,1)} %get-tuple-element., ...), custom_call_target="tpu_custom_call" | custom-call | bytes 13713408 | tf_op jit(solution)/shard_map/unpack/pallas_call | solution.py:1264
  320.2 0.0 copy-done.1
  320.2 3.2 fusion.1
  (6 shorter events, 0.1 us)
Async XLA Ops:
  0.7 4.9 %copy-start = (bf16[128,48,192]{0,2,1:T(8,128)(2,1)S(1)}, bf16[128,48,192]{0,2,1:T(8,128)(2,1)}, u32[]{:S(2)}) copy-start(bf16[128,48,192]{0,2,1:T(8,128)(2,1)} %param.46) | copy-start | bytes 7077892
  300.0 1.7 copy-start.4
  300.0 1.8 copy-start.2
  300.1 9.4 %copy-start.6 = (f32[2,128]{1,0:T(2,128)S(1)}, f32[2,128]{1,0:T(2,128)}, u32[]{:S(2)}) copy-start(f32[2,128]{1,0:T(2,128)} %param.44) | copy-start | bytes 3076
  300.1 10.7 %copy-start.3 = (f32[64,128]{1,0:T(8,128)S(1)}, f32[64,128]{1,0:T(8,128)}, u32[]{:S(2)}) copy-start(f32[64,128]{1,0:T(8,128)} %param.45) | copy-start | bytes 98308
  300.1 11.4 %copy-start.5 = (f32[8,64]{1,0:T(8,128)S(1)}, f32[8,64]{1,0:T(8,128)}, u32[]{:S(2)}) copy-start(f32[8,64]{1,0:T(8,128)} %param.43) | copy-start | bytes 6148
  313.3 6.9 %copy-start.1 = (bf16[8,96,192]{2,1,0:T(8,128)(2,1)S(1)}, bf16[8,96,192]{2,1,0:T(8,128)(2,1)}, u32[]{:S(2)}) copy-start(bf16[8,96,192]{2,1,0:T(8,128)(2,1)} %get-tuple-element.127) | copy-start | bytes 884740
